TPU v7x, 512 devices: a whole 4x8x8 slice. The times are simulated.
512 devices in a mesh: seq: 64 (over z, x, y_lo), tp: 8 (over y_hi, core).
Axes of the slice: x: 4, y: 8 (y_hi: 4, y_lo: 2; y = y_hi * 2 + y_lo), z: 8, core: 2. Of those that a mesh axis runs over, the one named last changes fastest.
Arguments:
- hidden_in: bfloat16 [8192, 5120], P('seq', 'tp'), may hold values from -6 to 6
- query_base: bfloat16 [8192, 5120], P('seq', 'tp'), may hold values from -10 to 10
- key_base: bfloat16 [8192, 5120], P('seq', 'tp'), may hold values from -10 to 10
- value_base: bfloat16 [8192, 5120], P('seq', 'tp'), may hold values from -6 to 6
- grad_out: bfloat16 [8192, 5120], P('seq', 'tp'), may hold values from -0.0625 to 0.0625
- adapter_down: bfloat16 [5120, 64], P('tp'), may hold values from -0.078125 to 0.078125
- adapter_up: bfloat16 [64, 5120], P(None, 'tp'), may hold values from -0.75 to 0.75
- tile_slot: int32 [8192], replicated, may hold values from 0 to 8191, as said below
- window_table: int32 [64, 4], P('seq'), may hold values from 0 to 63, as said below
Outputs:
- attended: bfloat16 [8192, 5120], P('seq', 'tp')
- grad_down: float32 [5120, 64], P('tp')
- grad_up: float32 [64, 5120], P(None, 'tp')
Inputs may be any that keep to these rules, and one draw needn't show every extreme that they name: `tile_slot`: A permutation of the 8192 positions. The 128 tokens of each aligned block of 128 rows send exactly 2 tokens into each tile. `window_table`: row p lists p first, then 4 - 1 distinct tiles of the form (p + d) mod 64 with d nonzero and between -2 and 2, chosen and ordered per row.
All inputs are finite; a program needn't handle non-finite values.
Results may differ from a plain program's by a relative error of at most 0.012.
Values may be sent and summed in bfloat16 or wider, within the bound.
No kernel may reach another device: no remote copies, remote signals or barrier semaphores. Data moves between devices by JAX's collectives and lax.ppermute only.
A program may use at most 64 MiB of HBM per device.

v0:
```python
import math

import jax
import jax.numpy as jnp
from jax import lax
from jax.sharding import PartitionSpec as P

HEAD_DIM = 128
REACH = 2


def shifted(shard, axis, by):
    devices = lax.axis_size(axis)
    return lax.ppermute(shard, axis, [(i, (i + by) % devices) for i in range(devices)])


def project_down(block, weight):
    partial_rows = jnp.dot(block, weight, preferred_element_type=jnp.float32)
    return lax.psum(partial_rows, "tp").astype(jnp.bfloat16)


def sum_low_grad(grad_query, adapter_up):
    partial_rows = lax.dot_general(
        grad_query, adapter_up, (((1,), (1,)), ((), ())), preferred_element_type=jnp.float32
    )
    return lax.psum(partial_rows, "tp").astype(jnp.bfloat16)


def token_product(left, right):
    return lax.dot_general(
        left, right, (((0,), (0,)), ((), ())), preferred_element_type=jnp.float32
    )


def local(
    hidden_in,
    query_base,
    key_base,
    value_base,
    grad_out,
    adapter_down,
    adapter_up,
    tile_slot,
    window_table,
):
    row_count = hidden_in.shape[0]
    local_width = hidden_in.shape[1]
    tile_count = lax.axis_size("seq")
    my_tile = lax.axis_index("seq")
    target_tile = tile_slot // row_count
    local_slot = tile_slot % row_count
    mine_targets = lax.dynamic_slice_in_dim(target_tile, my_tile * row_count, row_count)
    send_order = jnp.argsort(mine_targets, stable=True)
    arriving = jnp.nonzero(target_tile == my_tile, size=row_count)[0]
    arrive_slot = local_slot[arriving]
    counting = jnp.arange(row_count, dtype=jnp.int32)
    place = jnp.zeros((row_count,), jnp.int32).at[arrive_slot].set(counting)
    restore = jnp.zeros((row_count,), jnp.int32).at[send_order].set(counting)
    low_rank = project_down(hidden_in, adapter_down)
    query = (
        query_base.astype(jnp.float32)
        + jnp.dot(low_rank, adapter_up, preferred_element_type=jnp.float32)
    ).astype(jnp.bfloat16)
    query_recv, key_recv, value_recv, grad_recv = (
        lax.all_to_all(query[send_order], "seq", split_axis=0, concat_axis=0, tiled=True),
        lax.all_to_all(key_base[send_order], "seq", split_axis=0, concat_axis=0, tiled=True),
        lax.all_to_all(value_base[send_order], "seq", split_axis=0, concat_axis=0, tiled=True),
        lax.all_to_all(grad_out[send_order], "seq", split_axis=0, concat_axis=0, tiled=True),
    )
    query_tile = query_recv[place]
    key_tile = key_recv[place]
    value_tile = value_recv[place]
    grad_tile = grad_recv[place]
    key_value = jnp.stack([key_tile, value_tile])
    from_lower = []
    from_upper = []
    for offset in range(1, REACH + 1):
        from_lower.append(shifted(key_value, "seq", offset))
        from_upper.append(shifted(key_value, "seq", -offset))
    neighbor_stack = jnp.stack(from_lower[::-1] + [key_value] + from_upper)
    window_index = (window_table[0] - my_tile + REACH + tile_count) % tile_count
    window_tiles = neighbor_stack[window_index]
    window_keys = window_tiles[:, 0].reshape(-1, local_width)
    window_values = window_tiles[:, 1].reshape(-1, local_width)
    scale = 1.0 / math.sqrt(HEAD_DIM)

    def head_work(head_index):
        head_start = head_index * HEAD_DIM
        head_query = lax.dynamic_slice_in_dim(query_tile, head_start, HEAD_DIM, 1)
        head_keys = lax.dynamic_slice_in_dim(window_keys, head_start, HEAD_DIM, 1)
        head_values = lax.dynamic_slice_in_dim(window_values, head_start, HEAD_DIM, 1)
        head_grad = lax.dynamic_slice_in_dim(grad_tile, head_start, HEAD_DIM, 1)
        contract = (((1,), (1,)), ((), ()))
        scores = (
            lax.dot_general(head_query, head_keys, contract, preferred_element_type=jnp.float32)
            * scale
        )
        weights = jax.nn.softmax(scores, axis=-1)
        head_out = jnp.dot(
            weights.astype(jnp.bfloat16), head_values, preferred_element_type=jnp.float32
        ).astype(jnp.bfloat16)
        grad_weights = lax.dot_general(
            head_grad, head_values, contract, preferred_element_type=jnp.float32
        )
        row_dot = jnp.sum(weights * grad_weights, axis=-1, keepdims=True)
        grad_scores = (weights * (grad_weights - row_dot)).astype(jnp.bfloat16)
        grad_query = (
            jnp.dot(grad_scores, head_keys, preferred_element_type=jnp.float32) * scale
        ).astype(jnp.bfloat16)
        return (head_out, grad_query)

    head_outs, head_grads = lax.map(head_work, jnp.arange(local_width // HEAD_DIM, dtype=jnp.int32))
    out_tile = jnp.transpose(head_outs, (1, 0, 2)).reshape(row_count, local_width)
    grad_query_tile = jnp.transpose(head_grads, (1, 0, 2)).reshape(row_count, local_width)
    back_out, back_grad = (
        lax.all_to_all(out_tile[arrive_slot], "seq", split_axis=0, concat_axis=0, tiled=True),
        lax.all_to_all(
            grad_query_tile[arrive_slot], "seq", split_axis=0, concat_axis=0, tiled=True
        ),
    )
    grad_query = back_grad[restore]
    up_total = token_product(low_rank, grad_query)
    low_grad = sum_low_grad(grad_query, adapter_up)
    attended = back_out[restore]
    down_part = token_product(hidden_in, low_grad)
    grad_up, grad_down = lax.psum((up_total, down_part), "seq")
    return (attended, grad_down, grad_up)


def solution(mesh):
    return jax.shard_map(
        local,
        mesh=mesh,
        in_specs=(
            P("seq", "tp"),
            P("seq", "tp"),
            P("seq", "tp"),
            P("seq", "tp"),
            P("seq", "tp"),
            P("tp", None),
            P(None, "tp"),
            P(),
            P("seq", None),
        ),
        out_specs=(P("seq", "tp"), P("tp", None), P(None, "tp")),
        check_vma=False,
    )
```

profile of v0, /device:TPU:2, one launch (start us, length us, event | category | flops | bytes accessed | tf_op | source)
XLA Modules:
  0.0 839.0 jit_solution(7324716755973195393)
XLA Ops:
  7.2 1.5 convert_reduce_fusion
  8.8 2.5 sort.17
  12.9 14.9 %all-to-all-start.1 = ((bf16[64,2,640]{2,1,0:T(2,128)(2,1)}), bf16[64,2,640]{2,1,0:T(2,128)(2,1)S(1)}, u32[]{:S(2)}, u32[]{:S(2)}) async-start(bf16[64,2,640]{2,1,0:T(2,128)(2,1)} %all_to_all.51), calls=%async_computation.1 | async-start | bytes 327680 | tf_op jit(solution)/shard_map/all_to_all | solution.py:66
  28.6 57.0 %scatter_custom_fusion = s32[128]{0:T(128)S(1)} fusion(s32[8192]{0:T(1024)S(1)} %bitcast.62, s32[8192]{0:T(1024)S(1)} %ne.76, s32[]{:T(128)} %constant.102.clone.1), kind=kCustom, calls=%fused_computation.99 | custom fusion | flops 8192 | bytes 516 | tf_op jit(solution)/shard_map/scatter-add | solution.py:54
  86.9 1.1 gather_fusion.1
  89.7 29.3 %psum.28 = bf16[128,64]{0,1:T(8,128)(2,1)S(1)} all-reduce(f32[128,64]{0,1:T(8,128)S(1)} %fusion.41), channel_id=1, replica_groups=mesh['seq'=64,'tp'=8] {'tp'}, use_global_device_ids=true, to_apply=%region_0.1 | all-reduce | flops 8192 | bytes 49152 | tf_op jit(solution)/shard_map/psum | solution.py:19
  123.5 11.3 %all-to-all-start.2 = ((bf16[64,2,640]{2,1,0:T(2,128)(2,1)}), bf16[64,2,640]{2,1,0:T(2,128)(2,1)S(1)}, u32[]{:S(2)}, u32[]{:S(2)}) async-start(bf16[64,2,640]{2,1,0:T(2,128)(2,1)} %all_to_all.54), calls=%async_computation.2 | async-start | bytes 327680 | tf_op jit(solution)/shard_map/all_to_all | solution.py:67
  135.9 8.7 %all-to-all-done.2 = bf16[64,2,640]{2,1,0:T(2,128)(2,1)S(1)} async-done(((bf16[64,2,640]{2,1,0:T(2,128)(2,1)}), bf16[64,2,640]{2,1,0:T(2,128)(2,1)S(1)}, u32[]{:S(2)}, u32[]{:S(2)}) %all-to-all-start.2) | async-done | bytes 163872 | tf_op jit(solution)/shard_map/all_to_all | solution.py:67
  144.6 5.7 all-to-all-start
  152.3 3.4 collective-permute-start
  155.7 4.5 all-to-all-done
  160.2 6.5 all-to-all-start.3
  166.7 3.4 collective-permute-start.1
  170.1 3.4 collective-permute-start.2
  173.4 5.9 collective-permute-start.3
  180.3 1.5 gather_fusion.9
  182.9 1.0 bitcast_dynamic-update-slice_fusion.3
  184.0 1.0 bitcast_dynamic-update-slice_fusion.1
  187.8 17.8 %while.12 = (s32[]{:T(128)}, bf16[5,128,128]{1,2,0:T(8,128)(2,1)S(1)}, bf16[5,128,128]{1,2,0:T(8,128)(2,1)S(1)}, s32[5]{0:T(128)S(1)}, bf16[128,640]{1,0:T(8,128...) while((s32[]{:T(128)}, ...), condition=%wide.region_12.13_spmd, body=%wide.region_8.12_spmd.sunk | while | flops 68206208 | bytes 2760379 | solution.py:112
  189.9 1.0 multiply_reduce_fusion.2
  193.5 1.0 multiply_reduce_fusion.2
  197.1 1.0 multiply_reduce_fusion.2
  200.6 1.0 multiply_reduce_fusion.2
  204.2 1.0 multiply_reduce_fusion.2
  207.4 11.8 %all-to-all-start.5 = ((bf16[64,2,640]{2,1,0:T(2,128)(2,1)}), bf16[64,2,640]{2,1,0:T(2,128)(2,1)S(1)}, u32[]{:S(2)}, u32[]{:S(2)}) async-start(bf16[64,2,640]{2,1,0:T(2,128)(2,1)} %all_to_all.63), calls=%async_computation.5 | async-start | bytes 327680 | tf_op jit(solution)/shard_map/all_to_all | solution.py:117
  219.4 9.8 %all-to-all-done.5 = bf16[64,2,640]{2,1,0:T(2,128)(2,1)S(1)} async-done(((bf16[64,2,640]{2,1,0:T(2,128)(2,1)}), bf16[64,2,640]{2,1,0:T(2,128)(2,1)S(1)}, u32[]{:S(2)}, u32[]{:S(2)}) %all-to-all-start.5) | async-done | bytes 163872 | tf_op jit(solution)/shard_map/all_to_all | solution.py:117
  231.1 30.8 %psum.29 = bf16[128,64]{1,0:T(8,128)(2,1)S(1)} all-reduce(f32[128,64]{1,0:T(8,128)S(1)} %fusion.42), channel_id=1, replica_groups=mesh['seq'=64,'tp'=8] {'tp'}, use_global_device_ids=true, to_apply=%region_14.15 | all-reduce | flops 8192 | bytes 49152 | tf_op jit(solution)/shard_map/psum | solution.py:26
  263.9 17.1 %all_to_all.72 = bf16[64,2,640]{2,1,0:T(2,128)(2,1)S(1)} all-to-all(bf16[64,2,640]{2,1,0:T(2,128)(2,1)S(1)} %all_to_all.60), channel_id=1, replica_groups=mesh['seq'=64,'tp'=8] {'seq'}, dimensions={0} | all-to-all | bytes 327680 | tf_op jit(solution)/shard_map/all_to_all | solution.py:116
  281.0 1.5 gather_fusion.11
  282.6 546.4 %all-reduce.3.cloned.1.call-done = (f32[640,64]{0,1:T(8,128)}, f32[64,640]{1,0:T(8,128)}) async-done(((f32[640,64]{0,1:T(8,128)}, f32[64,640]{1,0:T(8,128)}), (f32[640,64]{0,1:T(8,128)}, f32[64,640]{1,0:T(8,128)})) %all-reduce.3.cloned.1.call-update) | async-done | bytes 327696 | tf_op jit(solution)/shard_map/psum | solution.py:126
  829.0 1.6 copy.51
  830.6 1.6 copy.52
  (135 shorter events, 32.8 us)
Async XLA Ops:
  7.2 4.1 copy-start
  7.2 79.4 %copy-start.3 = (bf16[128,640]{1,0:T(8,128)(2,1)S(1)}, bf16[128,640]{1,0:T(8,128)(2,1)}, u32[]{:S(2)}) copy-start(bf16[128,640]{1,0:T(8,128)(2,1)} %param.11) | copy-start | bytes 491524
  7.2 79.4 %copy-start.8 = (bf16[640,64]{0,1:T(8,128)(2,1)S(1)}, bf16[640,64]{0,1:T(8,128)(2,1)}, u32[]{:S(2)}) copy-start(bf16[640,64]{0,1:T(8,128)(2,1)} %param.16) | copy-start | bytes 245764
  11.3 76.8 %copy-start.1 = (bf16[128,640]{1,0:T(8,128)(2,1)S(1)}, bf16[128,640]{1,0:T(8,128)(2,1)}, u32[]{:S(2)}) copy-start(bf16[128,640]{1,0:T(8,128)(2,1)} %param.14) | copy-start | bytes 491524
  12.9 110.5 %all-to-all-start.1 = ((bf16[64,2,640]{2,1,0:T(2,128)(2,1)}), bf16[64,2,640]{2,1,0:T(2,128)(2,1)S(1)}, u32[]{:S(2)}, u32[]{:S(2)}) async-start(bf16[64,2,640]{2,1,0:T(2,128)(2,1)} %all_to_all.51), calls=%async_computation.1 | async-start | bytes 327680 | tf_op jit(solution)/shard_map/all_to_all | solution.py:66
  28.2 90.8 %copy-start.4 = (bf16[64,640]{1,0:T(8,128)(2,1)S(1)}, bf16[64,640]{1,0:T(8,128)(2,1)}, u32[]{:S(2)}) copy-start(bf16[64,640]{1,0:T(8,128)(2,1)} %param.17) | copy-start | bytes 245764
  28.2 90.8 %copy-start.5 = (bf16[128,640]{1,0:T(8,128)(2,1)S(1)}, bf16[128,640]{1,0:T(8,128)(2,1)}, u32[]{:S(2)}) copy-start(bf16[128,640]{1,0:T(8,128)(2,1)} %param.12) | copy-start | bytes 491524
  89.0 31.9 %copy-start.2 = (bf16[128,640]{1,0:T(8,128)(2,1)S(1)}, bf16[128,640]{1,0:T(8,128)(2,1)}, u32[]{:S(2)}) copy-start(bf16[128,640]{1,0:T(8,128)(2,1)} %param.15) | copy-start | bytes 491524
  123.5 21.1 %all-to-all-start.2 = ((bf16[64,2,640]{2,1,0:T(2,128)(2,1)}), bf16[64,2,640]{2,1,0:T(2,128)(2,1)S(1)}, u32[]{:S(2)}, u32[]{:S(2)}) async-start(bf16[64,2,640]{2,1,0:T(2,128)(2,1)} %all_to_all.54), calls=%async_computation.2 | async-start | bytes 327680 | tf_op jit(solution)/shard_map/all_to_all | solution.py:67
  144.6 15.6 %all-to-all-start = ((bf16[64,2,640]{2,1,0:T(2,128)(2,1)}), bf16[64,2,640]{2,1,0:T(2,128)(2,1)S(1)}, u32[]{:S(2)}, u32[]{:S(2)}) async-start(bf16[64,2,640]{2,1,0:T(2,128)(2,1)} %all_to_all.48), calls=%async_computation | async-start | bytes 327680 | tf_op jit(solution)/shard_map/all_to_all | solution.py:65
  151.3 15.3 %copy-start.9 = (s32[1,4]{1,0:T(1,128)S(1)}, s32[1,4]{1,0:T(1,128)}, u32[]{:S(2)}) copy-start(s32[1,4]{1,0:T(1,128)} %param.19) | copy-start | bytes 52
  152.3 29.6 %collective-permute-start = (bf16[2,128,640]{2,1,0:T(8,128)(2,1)S(1)}, bf16[2,128,640]{2,1,0:T(8,128)(2,1)}, u32[]{:S(2)}, u32[]{:S(2)}) collective-permute-start(bf16[2,128,640]{2,1,0:T(8,128)(2,1)S(1)} %pad_maximum_fusion), channel_id=1, source_target_pairs={{0,16},{8,24},{16,32},{24,40},{32,48},{40,56},{48,64},{56,72},{64,... | collective-permute-start | bytes 983048 | tf_op jit(solution)/shard_map/ppermute | solution.py:14
  160.2 20.1 %all-to-all-start.3 = ((bf16[64,2,640]{2,1,0:T(2,128)(2,1)}), bf16[64,2,640]{2,1,0:T(2,128)(2,1)S(1)}, u32[]{:S(2)}, u32[]{:S(2)}) async-start(bf16[64,2,640]{2,1,0:T(2,128)(2,1)} %all_to_all.57), calls=%async_computation.3 | async-start | bytes 327680 | tf_op jit(solution)/shard_map/all_to_all | solution.py:68
  166.7 16.2 %collective-permute-start.1 = (bf16[2,128,640]{2,1,0:T(8,128)(2,1)S(1)}, bf16[2,128,640]{2,1,0:T(8,128)(2,1)}, u32[]{:S(2)}, u32[]{:S(2)}) collective-permute-start(bf16[2,128,640]{2,1,0:T(8,128)(2,1)S(1)} %pad_maximum_fusion), channel_id=1, source_target_pairs={{0,8},{8,16},{16,24},{24,32},{32,40},{40,48},{48,56},{56,64},{64,7... | collective-permute-start | bytes 983048 | tf_op jit(solution)/shard_map/ppermute | solution.py:14
  170.1 13.9 %collective-permute-start.2 = (bf16[2,128,640]{2,1,0:T(8,128)(2,1)S(1)}, bf16[2,128,640]{2,1,0:T(8,128)(2,1)}, u32[]{:S(2)}, u32[]{:S(2)}) collective-permute-start(bf16[2,128,640]{2,1,0:T(8,128)(2,1)S(1)} %pad_maximum_fusion), channel_id=1, source_target_pairs={{0,504},{8,0},{16,8},{24,16},{32,24},{40,32},{48,40},{56,48},{64,5... | collective-permute-start | bytes 983048 | tf_op jit(solution)/shard_map/ppermute | solution.py:14
  173.4 11.6 %collective-permute-start.3 = (bf16[2,128,640]{2,1,0:T(8,128)(2,1)S(1)}, bf16[2,128,640]{2,1,0:T(8,128)(2,1)}, u32[]{:S(2)}, u32[]{:S(2)}) collective-permute-start(bf16[2,128,640]{2,1,0:T(8,128)(2,1)S(1)} %pad_maximum_fusion), channel_id=1, source_target_pairs={{0,496},{8,504},{16,0},{24,8},{32,16},{40,24},{48,32},{56,40},{64,... | collective-permute-start | bytes 983048 | tf_op jit(solution)/shard_map/ppermute | solution.py:14
  186.8 0.9 copy-start.6
  186.8 1.0 copy-start.7
  207.4 21.7 %all-to-all-start.5 = ((bf16[64,2,640]{2,1,0:T(2,128)(2,1)}), bf16[64,2,640]{2,1,0:T(2,128)(2,1)S(1)}, u32[]{:S(2)}, u32[]{:S(2)}) async-start(bf16[64,2,640]{2,1,0:T(2,128)(2,1)} %all_to_all.63), calls=%async_computation.5 | async-start | bytes 327680 | tf_op jit(solution)/shard_map/all_to_all | solution.py:117
  219.3 609.7 %all-reduce.3.cloned.1.call-start = ((), (), s32[]{:S(2)}) async-start(), calls=%async_computation.6 | async-start | bytes 655360 | tf_op jit(solution)/shard_map/psum | solution.py:126
Sparse Core Ops, SparseCore 0:
  262.9 566.0 all-reduce.2
where the time goes:
time: 840 us; the launch traced here: 839 us
  waiting for transfers between devices  569 us (68%)
  blocking collectives  77.1 us (9%)
  starting transfers between devices  66.1 us (8%)
  other arithmetic  63.7 us (8%)
  local copies, waits for them, and re-layouts  33.2 us (4%)
  between operations  14.5 us (2%)
  matrix products  11.5 us (1%)
    psum x1, waiting for transfers between devices, local(): grad_up, grad_down = lax.psum((up_total, down_part), 'seq')  546 us
    scatter-add x1, other arithmetic, local(): arriving = jnp.nonzero(target_tile == my_tile, size=row_count)[0]  57 us
    psum x1, blocking collectives, sum_low_grad(): return lax.psum(partial_rows, 'tp').astype(jnp.bfloat16)  30.8 us
    psum x1, blocking collectives, project_down(): return lax.psum(partial_rows, 'tp').astype(jnp.bfloat16)  29.3 us
    all_to_all x1, blocking collectives, local(): lax.all_to_all(out_tile[arrive_slot], 'seq', split_axis=0, concat_axis=0,...  17.1 us
  transfers between devices with their start and end apart: 10, of which 4 were waited for; matrix products, arithmetic and copies ran while one was open for 9% of the time, Pallas kernels for 0%

commit v1 on v0

v1 whole, which is shorter than its diff:
```python
import functools
import math

import jax
import jax.numpy as jnp
from jax import lax
from jax.experimental import pallas as pl
from jax.experimental.pallas import tpu as pltpu
from jax.sharding import PartitionSpec as P

HEAD_DIM = 128
REACH = 2
VMEM_BYTES = 48 * 1024 * 1024
NT = (((1,), (1,)), ((), ()))
NN = (((1,), (0,)), ((), ()))
TN = (((0,), (0,)), ((), ()))


def product(left, right, dims=NN):
    return lax.dot_general(left, right, dims, preferred_element_type=jnp.float32)


def shifted(shard, by):
    devices = lax.axis_size("seq")
    return lax.ppermute(shard, "seq", [(i, (i + by) % devices) for i in range(devices)])


def swap(blocks, axis):
    return lax.all_to_all(blocks, axis, split_axis=0, concat_axis=0, tiled=True)


def call(body, out_shape, prefetch=(), operands=(), in_specs=None, cost=None):
    def whole(shape):
        return pl.BlockSpec(shape, lambda i, *_: (0,) * len(shape))

    outs = out_shape if isinstance(out_shape, (list, tuple)) else [out_shape]
    specs = in_specs or [None] * len(operands)
    return pl.pallas_call(
        body,
        out_shape=out_shape,
        grid_spec=pltpu.PrefetchScalarGridSpec(
            num_scalar_prefetch=len(prefetch),
            grid=(1,),
            in_specs=[s or whole(o.shape) for s, o in zip(specs, operands)],
            out_specs=jax.tree.map(lambda o: whole(o.shape), out_shape),
        ),
        compiler_params=pltpu.CompilerParams(vmem_limit_bytes=VMEM_BYTES),
        cost_estimate=cost,
    )(*prefetch, *operands)


def low_rank_kernel(hidden, down_t, parts):
    part = product(down_t[...], hidden[...], NT)
    for k in range(parts.shape[0]):
        parts[k] = part


def order_kernel(me, slots, key, value, order, send):
    tokens = order.shape[0]
    target = slots[0] // tokens
    rows = lax.broadcasted_iota(jnp.int32, (tokens, tokens), 0)
    cols = lax.broadcasted_iota(jnp.int32, (tokens, tokens), 1)
    spread = jnp.broadcast_to(target, (tokens, tokens))
    target_col = jnp.sum(jnp.where(rows == cols, spread, 0), axis=1, keepdims=True)
    earlier = jnp.logical_and(target_col == spread, rows < cols)
    rank = jnp.sum(jnp.where(earlier, 1, 0), axis=0, keepdims=True)
    place = target * (tokens // lax.axis_size("seq")) + rank
    one_hot = jnp.where(rows == place, 1.0, 0.0).astype(jnp.bfloat16)
    order[...] = one_hot
    width = key.shape[1]
    send[:, :width] = product(one_hot, key[...]).astype(jnp.bfloat16)
    send[:, width:] = product(one_hot, value[...]).astype(jnp.bfloat16)


def query_kernel(parts, query_base, grad, hidden, up, order, send):
    tokens, width = query_base.shape
    rank = up.shape[0]
    total = parts[0]
    for k in range(1, parts.shape[0]):
        total = total + parts[k]
    low_t = total.astype(jnp.bfloat16)
    query = (query_base[...].astype(jnp.float32) + product(low_t, up[...], TN)).astype(jnp.bfloat16)
    one_hot = order[...]
    send[:, :width] = product(one_hot, query).astype(jnp.bfloat16)
    send[:, width : 2 * width] = product(one_hot, grad[...]).astype(jnp.bfloat16)
    send[:, 2 * width : 3 * width] = product(one_hot, hidden[...]).astype(jnp.bfloat16)
    send[:, 3 * width : 3 * width + rank] = product(one_hot, low_t, NT).astype(jnp.bfloat16)
    send[:, 3 * width + rank :] = jnp.zeros((tokens, send.shape[1] - 3 * width - rank), jnp.bfloat16)


def attend_kernel(tiles, me, window, kv_own, kv_a, kv_b, kv_c, kv_d, rows, up, out, low_parts, up_part):
    tokens = kv_own.shape[0]
    width = out.shape[1]
    rank = up.shape[0]
    missing = jnp.int32(6)
    for k in range(1, 4):
        away = lax.rem(window[k] - me[0] + tiles, tiles)
        missing = missing - jnp.where(away <= REACH, away + 1, away - (tiles - REACH))
    near = (kv_own, kv_a, kv_b, kv_c, kv_d)

    scale = 1.0 / math.sqrt(HEAD_DIM)
    low = rows[:, 3 * width : 3 * width + rank]
    low_total = jnp.zeros((rank, tokens), jnp.float32)
    for h in range(width // HEAD_DIM):
        columns = slice(h * HEAD_DIM, (h + 1) * HEAD_DIM)
        value_columns = slice(width + h * HEAD_DIM, width + (h + 1) * HEAD_DIM)
        keys = jnp.concatenate(
            [kv_own[:, columns]]
            + [jnp.where(missing < k, near[k + 1][:, columns], near[k][:, columns]) for k in (1, 2, 3)],
            axis=0,
        )
        values = jnp.concatenate(
            [kv_own[:, value_columns]]
            + [jnp.where(missing < k, near[k + 1][:, value_columns], near[k][:, value_columns]) for k in (1, 2, 3)],
            axis=0,
        )
        query = rows[:, columns]
        grad = rows[:, value_columns]
        scores = product(query, keys, NT) * scale
        exps = jnp.exp(scores - jnp.max(scores, axis=-1, keepdims=True))
        weights = exps / jnp.sum(exps, axis=-1, keepdims=True)
        out[:, columns] = product(weights.astype(jnp.bfloat16), values).astype(jnp.bfloat16)
        grad_weights = product(grad, values, NT)
        row_dot = jnp.sum(weights * grad_weights, axis=-1, keepdims=True)
        grad_scores = (weights * (grad_weights - row_dot)).astype(jnp.bfloat16)
        grad_query = (product(grad_scores, keys) * scale).astype(jnp.bfloat16)
        low_total = low_total + product(up[:, columns], grad_query, NT)
        up_part[:, columns] = product(low, grad_query, TN)
    for k in range(low_parts.shape[0]):
        low_parts[k] = low_total


def down_kernel(parts, hidden, down_part):
    total = parts[0]
    for k in range(1, parts.shape[0]):
        total = total + parts[k]
    down_part[...] = product(total.astype(jnp.bfloat16), hidden[...])


def restore_kernel(order, back, attended):
    attended[...] = product(order[...], back[...], TN).astype(jnp.bfloat16)


def local(
    hidden_in,
    query_base,
    key_base,
    value_base,
    grad_out,
    adapter_down,
    adapter_up,
    tile_slot,
    window_table,
):
    tokens, width = hidden_in.shape
    rank = adapter_up.shape[0]
    tiles = lax.axis_size("seq")
    group = lax.axis_size("tp")
    peer = tokens // tiles
    bf16, f32 = jnp.bfloat16, jnp.float32
    shape = jax.ShapeDtypeStruct
    me = lax.axis_index("seq").astype(jnp.int32).reshape(1)

    low_parts = swap(
        call(low_rank_kernel, shape((group, rank, tokens), f32), (), (hidden_in, adapter_down.T)), "tp"
    )
    order, kv_send = call(
        order_kernel,
        [shape((tokens, tokens), bf16), shape((tokens, 2 * width), bf16)],
        (me,),
        (tile_slot.reshape(tiles, 1, tokens), key_base, value_base),
        [pl.BlockSpec((1, 1, tokens), lambda i, me: (me[0], 0, 0)), None, None],
    )
    kv_own = swap(kv_send.reshape(tiles, peer, -1), "seq").reshape(tokens, -1)
    kv_near = [shifted(kv_own, by) for by in (2, 1, -1, -2)]
    row_send = call(
        query_kernel,
        shape((tokens, 3 * width + 128), bf16),
        (),
        (low_parts, query_base, grad_out, hidden_in, adapter_up, order),
    )
    rows = swap(row_send.reshape(tiles, peer, -1), "seq").reshape(tokens, -1)
    out_tile, low_grad_parts, up_part = call(
        functools.partial(attend_kernel, tiles),
        [shape((tokens, width), bf16), shape((group, rank, tokens), f32), shape((rank, width), f32)],
        (me, window_table[0]),
        (kv_own, *kv_near, rows, adapter_up),
    )
    low_grad_parts = swap(low_grad_parts, "tp")
    up_rows = swap(up_part.reshape(rank, 1, width), "seq")
    back = swap(out_tile.reshape(tiles, peer, width), "seq").reshape(tokens, width)
    down_part = call(
        down_kernel,
        shape((rank, width), f32),
        (),
        (low_grad_parts, rows),
        [None, pl.BlockSpec((tokens, width), lambda i: (0, 2))],
    )
    down_rows = swap(down_part.reshape(rank, 1, width), "seq")
    sums = jnp.concatenate([jnp.sum(up_rows, axis=0), jnp.sum(down_rows, axis=0)], axis=-1)
    totals = swap(jnp.broadcast_to(sums[None], (tiles, 1, 2 * width)), "seq").reshape(rank, 2 * width)
    attended = call(restore_kernel, shape((tokens, width), bf16), (), (order, back))
    return attended, totals[:, width:].T, totals[:, :width]


def solution(mesh):
    return jax.shard_map(
        local,
        mesh=mesh,
        in_specs=(
            P("seq", "tp"),
            P("seq", "tp"),
            P("seq", "tp"),
            P("seq", "tp"),
            P("seq", "tp"),
            P("tp", None),
            P(None, "tp"),
            P(),
            P("seq", None),
        ),
        out_specs=(P("seq", "tp"), P("tp", None), P(None, "tp")),
        check_vma=False,
    )
```

time: 840 us -> 174 us (0.21)
  the two profiles are of different devices: /device:TPU:2 before, /device:TPU:8 now
where the time goes in v1:
time: 174 us; the launch traced here: 173 us
  waiting for transfers between devices  84.7 us (49%)
  starting transfers between devices  70.9 us (41%)
  local copies, waits for them, and re-layouts  8.32 us (5%)
  Pallas kernels  8.08 us (5%)
    all_to_all x8, waiting for transfers between devices, swap(): return lax.all_to_all(blocks, axis, split_axis=0, concat_axis=0, tiled=True)  78.3 us
    all_to_all x8, starting transfers between devices, swap(): return lax.all_to_all(blocks, axis, split_axis=0, concat_axis=0, tiled=True)  55.2 us
    ppermute x4, starting transfers between devices, shifted(): lax.ppermute(shard, 'seq', [(i, (i + by) % devices) for i in range(device...  15.7 us
    pallas_call x6, Pallas kernels, call(): pl.pallas_call(body, out_shape=out_shape, grid_spec=pltpu.PrefetchScalarG...  8.08 us
    ppermute x4, waiting for transfers between devices, shifted(): lax.ppermute(shard, 'seq', [(i, (i + by) % devices) for i in range(device...  6.39 us
  transfers between devices with their start and end apart: 12, of which 11 were waited for; matrix products, arithmetic and copies ran while one was open for 3% of the time, Pallas kernels for 1%

profile of v1, /device:TPU:8, one launch (start us, length us, event | category | flops | bytes accessed | tf_op | source)
XLA Modules:
  0.0 173.1 jit_solution(3664914256480726296)
XLA Ops:
  0.6 0.9 copy-done
  1.6 0.9 copy-done.7
  2.4 0.9 shard_map.113
  3.4 6.3 %all-to-all-start.1 = ((f32[8,64,128]{2,1,0:T(8,128)}), f32[8,64,128]{2,1,0:T(8,128)S(1)}, u32[]{:S(2)}, u32[]{:S(2)}) async-start(f32[8,64,128]{2,1,0:T(8,128)} %shard_map.113), calls=%async_computation.1 | async-start | bytes 524288 | tf_op jit(solution)/shard_map/all_to_all | solution.py:29
  10.1 0.9 reshape.46
  11.0 11.5 %all-to-all-done.1.parts = f32[8,64,128]{2,1,0:T(8,128)S(1)} async-done(((f32[8,64,128]{2,1,0:T(8,128)}), f32[8,64,128]{2,1,0:T(8,128)S(1)}, u32[]{:S(2)}, u32[]{:S(2)}) %all-to-all-start.1) | async-done | bytes 262176 | tf_op jit(solution)/shard_map/all_to_all | solution.py:29
  22.5 14.7 %all-to-all-start = ((bf16[64,2,1280]{2,1,0:T(2,128)(2,1)}), bf16[64,2,1280]{2,1,0:T(2,128)(2,1)S(1)}, u32[]{:S(2)}, u32[]{:S(2)}) async-start(bf16[64,2,1280]{2,1,0:T(2,128)(2,1)} %reshape.46), calls=%async_computation | async-start | bytes 655360 | tf_op jit(solution)/shard_map/all_to_all | solution.py:29
  37.8 1.1 reshape.48
  38.9 11.0 %all-to-all-done = bf16[64,2,1280]{2,1,0:T(2,128)(2,1)S(1)} async-done(((bf16[64,2,1280]{2,1,0:T(2,128)(2,1)}), bf16[64,2,1280]{2,1,0:T(2,128)(2,1)S(1)}, u32[]{:S(2)}, u32[]{:S(2)}) %all-to-all-start) | async-done | bytes 327712 | tf_op jit(solution)/shard_map/all_to_all | solution.py:29
  49.9 5.1 %all-to-all-start.2 = ((bf16[64,2,2048]{2,1,0:T(2,128)(2,1)}), bf16[64,2,2048]{2,1,0:T(2,128)(2,1)S(1)}, u32[]{:S(2)}, u32[]{:S(2)}) async-start(bf16[64,2,2048]{2,1,0:T(2,128)(2,1)} %reshape.48), calls=%async_computation.2 | async-start | bytes 1048576 | tf_op jit(solution)/shard_map/all_to_all | solution.py:29
  55.1 7.0 %collective-permute-start.3 = (bf16[128,1280]{1,0:T(8,128)(2,1)S(1)}, bf16[128,1280]{1,0:T(8,128)(2,1)S(1)}, u32[]{:S(2)}, u32[]{:S(2)}) collective-permute-start(bf16[128,1280]{1,0:T(8,128)(2,1)S(1)} %reshape.47.kv_own), channel_id=1, source_target_pairs={{0,496},{8,504},{16,0},{24,8},{32,16},{40,24},{48,32},{56,40},{64,... | collective-permute-start | bytes 983048 | tf_op jit(solution)/shard_map/ppermute | solution.py:25
  62.2 2.5 %collective-permute-start.2 = (bf16[128,1280]{1,0:T(8,128)(2,1)S(1)}, bf16[128,1280]{1,0:T(8,128)(2,1)S(1)}, u32[]{:S(2)}, u32[]{:S(2)}) collective-permute-start(bf16[128,1280]{1,0:T(8,128)(2,1)S(1)} %reshape.47.kv_own), channel_id=1, source_target_pairs={{0,504},{8,0},{16,8},{24,16},{32,24},{40,32},{48,40},{56,48},{64,5... | collective-permute-start | bytes 983048 | tf_op jit(solution)/shard_map/ppermute | solution.py:25
  64.6 4.3 %collective-permute-start.1 = (bf16[128,1280]{1,0:T(8,128)(2,1)S(1)}, bf16[128,1280]{1,0:T(8,128)(2,1)S(1)}, u32[]{:S(2)}, u32[]{:S(2)}) collective-permute-start(bf16[128,1280]{1,0:T(8,128)(2,1)S(1)} %reshape.47.kv_own), channel_id=1, source_target_pairs={{0,8},{8,16},{16,24},{24,32},{32,40},{40,48},{48,56},{56,64},{64,7... | collective-permute-start | bytes 983048 | tf_op jit(solution)/shard_map/ppermute | solution.py:25
  68.9 1.9 %collective-permute-start = (bf16[128,1280]{1,0:T(8,128)(2,1)S(1)}, bf16[128,1280]{1,0:T(8,128)(2,1)S(1)}, u32[]{:S(2)}, u32[]{:S(2)}) collective-permute-start(bf16[128,1280]{1,0:T(8,128)(2,1)S(1)} %reshape.47.kv_own), channel_id=1, source_target_pairs={{0,16},{8,24},{16,32},{24,40},{32,48},{40,56},{48,64},{56,72},{64,... | collective-permute-start | bytes 983048 | tf_op jit(solution)/shard_map/ppermute | solution.py:25
  70.8 3.8 %all-to-all-done.2 = bf16[64,2,2048]{2,1,0:T(2,128)(2,1)S(1)} async-done(((bf16[64,2,2048]{2,1,0:T(2,128)(2,1)}), bf16[64,2,2048]{2,1,0:T(2,128)(2,1)S(1)}, u32[]{:S(2)}, u32[]{:S(2)}) %all-to-all-start.2) | async-done | bytes 524320 | tf_op jit(solution)/shard_map/all_to_all | solution.py:29
  74.9 4.5 %collective-permute-done.3.kv_d = bf16[128,1280]{1,0:T(8,128)(2,1)S(1)} collective-permute-done((bf16[128,1280]{1,0:T(8,128)(2,1)S(1)}, bf16[128,1280]{1,0:T(8,128)(2,1)S(1)}, u32[]{:S(2)}, u32[]{:S(2)}) %collective-permute-start.3) | collective-permute-done | bytes 327712 | tf_op jit(solution)/shard_map/ppermute | solution.py:25
  79.5 1.8 %collective-permute-done.kv_a = bf16[128,1280]{1,0:T(8,128)(2,1)S(1)} collective-permute-done((bf16[128,1280]{1,0:T(8,128)(2,1)S(1)}, bf16[128,1280]{1,0:T(8,128)(2,1)S(1)}, u32[]{:S(2)}, u32[]{:S(2)}) %collective-permute-start) | collective-permute-done | bytes 327712 | tf_op jit(solution)/shard_map/ppermute | solution.py:25
  81.3 5.2 %shard_map.115 = (bf16[128,640]{1,0:T(8,128)(2,1)S(1)}, f32[8,64,128]{2,1,0:T(8,128)}, f32[64,640]{1,0:T(8,128)S(1)}) custom-call(s32[1]{0:T(128)} %bitcast.me, s32[4]{0:T(128)S(1)} %bitcast.15, bf16[128,1280]{1,0:T(8,128)(2,1)S(1)} %reshape.47.kv_own, bf16[128,1280]{1,0:T(8,128)(2,1)S(1)} %collective-permute-done.kv_a, ...), custom_call_target="tpu_custom_call" | custom-call | tf_op jit(solution)/shard_map/pallas_call | solution.py:38
  86.6 3.8 %all-to-all-start.5 = ((f32[8,64,128]{2,1,0:T(8,128)}), f32[8,64,128]{2,1,0:T(8,128)S(1)}, u32[]{:S(2)}, u32[]{:S(2)}) async-start(f32[8,64,128]{2,1,0:T(8,128)} %get-tuple-element.12), calls=%async_computation.5 | async-start | bytes 524288 | tf_op jit(solution)/shard_map/all_to_all | solution.py:29
  90.3 0.8 copy.12
  91.2 10.5 %all-to-all-done.5.parts = f32[8,64,128]{2,1,0:T(8,128)S(1)} async-done(((f32[8,64,128]{2,1,0:T(8,128)}), f32[8,64,128]{2,1,0:T(8,128)S(1)}, u32[]{:S(2)}, u32[]{:S(2)}) %all-to-all-start.5) | async-done | bytes 262176 | tf_op jit(solution)/shard_map/all_to_all | solution.py:29
  101.7 10.9 %all-to-all-start.4 = ((f32[64,1,640]{2,1,0:T(1,128)}), f32[64,1,640]{2,1,0:T(1,128)S(1)}, u32[]{:S(2)}, u32[]{:S(2)}) async-start(f32[64,1,640]{2,1,0:T(1,128)} %copy.12), calls=%async_computation.4 | async-start | bytes 327680 | tf_op jit(solution)/shard_map/all_to_all | solution.py:29
  112.7 0.8 copy.13
  113.6 9.7 %all-to-all-done.4 = f32[64,1,640]{2,1,0:T(1,128)S(1)} async-done(((f32[64,1,640]{2,1,0:T(1,128)}), f32[64,1,640]{2,1,0:T(1,128)S(1)}, u32[]{:S(2)}, u32[]{:S(2)}) %all-to-all-start.4) | async-done | bytes 163872 | tf_op jit(solution)/shard_map/all_to_all | solution.py:29
  123.3 4.8 %all-to-all-start.6 = ((f32[64,1,640]{2,1,0:T(1,128)}), f32[64,1,640]{2,1,0:T(1,128)S(1)}, u32[]{:S(2)}, u32[]{:S(2)}) async-start(f32[64,1,640]{2,1,0:T(1,128)} %copy.13), calls=%async_computation.6 | async-start | bytes 327680 | tf_op jit(solution)/shard_map/all_to_all | solution.py:29
  128.8 10.0 %all-to-all-done.6 = f32[64,1,640]{2,1,0:T(1,128)S(1)} async-done(((f32[64,1,640]{2,1,0:T(1,128)}), f32[64,1,640]{2,1,0:T(1,128)S(1)}, u32[]{:S(2)}, u32[]{:S(2)}) %all-to-all-start.6) | async-done | bytes 163872 | tf_op jit(solution)/shard_map/all_to_all | solution.py:29
  138.8 4.8 %all-to-all-start.3 = ((bf16[64,2,640]{2,1,0:T(2,128)(2,1)}), bf16[64,2,640]{2,1,0:T(2,128)(2,1)S(1)}, u32[]{:S(2)}, u32[]{:S(2)}) async-start(bf16[64,2,640]{2,1,0:T(2,128)(2,1)} %reshape.50), calls=%async_computation.3 | async-start | bytes 327680 | tf_op jit(solution)/shard_map/all_to_all | solution.py:29
  144.0 10.4 %all-to-all-done.3 = bf16[64,2,640]{2,1,0:T(2,128)(2,1)S(1)} async-done(((bf16[64,2,640]{2,1,0:T(2,128)(2,1)}), bf16[64,2,640]{2,1,0:T(2,128)(2,1)S(1)}, u32[]{:S(2)}, u32[]{:S(2)}) %all-to-all-start.3) | async-done | bytes 163872 | tf_op jit(solution)/shard_map/all_to_all | solution.py:29
  154.4 0.9 broadcast_in_dim.9
  155.3 4.8 %all-to-all-start.7 = ((f32[64,1,1280]{2,1,0:T(1,128)}), f32[64,1,1280]{2,1,0:T(1,128)S(1)}, u32[]{:S(2)}, u32[]{:S(2)}) async-start(f32[64,1,1280]{2,1,0:T(1,128)} %broadcast_in_dim.9), calls=%async_computation.7 | async-start | bytes 655360 | tf_op jit(solution)/shard_map/all_to_all | solution.py:29
  160.2 0.9 shard_map.116
  161.1 11.2 %all-to-all-done.7 = f32[64,1,1280]{2,1,0:T(1,128)S(1)} async-done(((f32[64,1,1280]{2,1,0:T(1,128)}), f32[64,1,1280]{2,1,0:T(1,128)S(1)}, u32[]{:S(2)}, u32[]{:S(2)}) %all-to-all-start.7) | async-done | bytes 327712 | tf_op jit(solution)/shard_map/all_to_all | solution.py:29
  (34 shorter events, 3.3 us)
Async XLA Ops:
  0.6 0.9 copy-start
  1.5 0.9 copy-start.7
  3.4 6.3 %copy-start.3 = (bf16[128,640]{1,0:T(8,128)(2,1)S(1)}, bf16[128,640]{1,0:T(8,128)(2,1)}, u32[]{:S(2)}) copy-start(bf16[128,640]{1,0:T(8,128)(2,1)} %key.1) | copy-start | bytes 491524
  3.4 6.3 %copy-start.4 = (bf16[128,640]{1,0:T(8,128)(2,1)S(1)}, bf16[128,640]{1,0:T(8,128)(2,1)}, u32[]{:S(2)}) copy-start(bf16[128,640]{1,0:T(8,128)(2,1)} %value.1) | copy-start | bytes 491524
  3.4 6.4 %copy-start.8 = (s32[8192]{0:T(1024)S(1)}, s32[8192]{0:T(1024)}, u32[]{:S(2)}) copy-start(s32[8192]{0:T(1024)} %param.16) | copy-start | bytes 98308
  3.4 19.1 %all-to-all-start.1 = ((f32[8,64,128]{2,1,0:T(8,128)}), f32[8,64,128]{2,1,0:T(8,128)S(1)}, u32[]{:S(2)}, u32[]{:S(2)}) async-start(f32[8,64,128]{2,1,0:T(8,128)} %shard_map.113), calls=%async_computation.1 | async-start | bytes 524288 | tf_op jit(solution)/shard_map/all_to_all | solution.py:29
  11.0 26.3 %copy-start.1 = (bf16[128,640]{1,0:T(8,128)(2,1)S(1)}, bf16[128,640]{1,0:T(8,128)(2,1)}, u32[]{:S(2)}) copy-start(bf16[128,640]{1,0:T(8,128)(2,1)} %hidden.3) | copy-start | bytes 491524
  11.0 26.3 %copy-start.2 = (bf16[64,640]{1,0:T(8,128)(2,1)S(1)}, bf16[64,640]{1,0:T(8,128)(2,1)}, u32[]{:S(2)}) copy-start(bf16[64,640]{1,0:T(8,128)(2,1)} %up.3) | copy-start | bytes 245764
  11.0 26.3 %copy-start.5 = (bf16[128,640]{1,0:T(8,128)(2,1)S(1)}, bf16[128,640]{1,0:T(8,128)(2,1)}, u32[]{:S(2)}) copy-start(bf16[128,640]{1,0:T(8,128)(2,1)} %query_base.1) | copy-start | bytes 491524
  11.0 26.3 %copy-start.6 = (bf16[128,640]{1,0:T(8,128)(2,1)S(1)}, bf16[128,640]{1,0:T(8,128)(2,1)}, u32[]{:S(2)}) copy-start(bf16[128,640]{1,0:T(8,128)(2,1)} %grad.1) | copy-start | bytes 491524
  22.5 27.5 %all-to-all-start = ((bf16[64,2,1280]{2,1,0:T(2,128)(2,1)}), bf16[64,2,1280]{2,1,0:T(2,128)(2,1)S(1)}, u32[]{:S(2)}, u32[]{:S(2)}) async-start(bf16[64,2,1280]{2,1,0:T(2,128)(2,1)} %reshape.46), calls=%async_computation | async-start | bytes 655360 | tf_op jit(solution)/shard_map/all_to_all | solution.py:29
  49.9 24.8 %all-to-all-start.2 = ((bf16[64,2,2048]{2,1,0:T(2,128)(2,1)}), bf16[64,2,2048]{2,1,0:T(2,128)(2,1)S(1)}, u32[]{:S(2)}, u32[]{:S(2)}) async-start(bf16[64,2,2048]{2,1,0:T(2,128)(2,1)} %reshape.48), calls=%async_computation.2 | async-start | bytes 1048576 | tf_op jit(solution)/shard_map/all_to_all | solution.py:29
  55.1 24.2 %collective-permute-start.3 = (bf16[128,1280]{1,0:T(8,128)(2,1)S(1)}, bf16[128,1280]{1,0:T(8,128)(2,1)S(1)}, u32[]{:S(2)}, u32[]{:S(2)}) collective-permute-start(bf16[128,1280]{1,0:T(8,128)(2,1)S(1)} %reshape.47.kv_own), channel_id=1, source_target_pairs={{0,496},{8,504},{16,0},{24,8},{32,16},{40,24},{48,32},{56,40},{64,... | collective-permute-start | bytes 983048 | tf_op jit(solution)/shard_map/ppermute | solution.py:25
  62.2 17.2 %collective-permute-start.2 = (bf16[128,1280]{1,0:T(8,128)(2,1)S(1)}, bf16[128,1280]{1,0:T(8,128)(2,1)S(1)}, u32[]{:S(2)}, u32[]{:S(2)}) collective-permute-start(bf16[128,1280]{1,0:T(8,128)(2,1)S(1)} %reshape.47.kv_own), channel_id=1, source_target_pairs={{0,504},{8,0},{16,8},{24,16},{32,24},{40,32},{48,40},{56,48},{64,5... | collective-permute-start | bytes 983048 | tf_op jit(solution)/shard_map/ppermute | solution.py:25
  64.6 14.8 %collective-permute-start.1 = (bf16[128,1280]{1,0:T(8,128)(2,1)S(1)}, bf16[128,1280]{1,0:T(8,128)(2,1)S(1)}, u32[]{:S(2)}, u32[]{:S(2)}) collective-permute-start(bf16[128,1280]{1,0:T(8,128)(2,1)S(1)} %reshape.47.kv_own), channel_id=1, source_target_pairs={{0,8},{8,16},{16,24},{24,32},{32,40},{40,48},{48,56},{56,64},{64,7... | collective-permute-start | bytes 983048 | tf_op jit(solution)/shard_map/ppermute | solution.py:25
  68.9 12.4 %collective-permute-start = (bf16[128,1280]{1,0:T(8,128)(2,1)S(1)}, bf16[128,1280]{1,0:T(8,128)(2,1)S(1)}, u32[]{:S(2)}, u32[]{:S(2)}) collective-permute-start(bf16[128,1280]{1,0:T(8,128)(2,1)S(1)} %reshape.47.kv_own), channel_id=1, source_target_pairs={{0,16},{8,24},{16,32},{24,40},{32,48},{40,56},{48,64},{56,72},{64,... | collective-permute-start | bytes 983048 | tf_op jit(solution)/shard_map/ppermute | solution.py:25
  74.9 6.4 %copy-start.9 = (s32[1,4]{1,0:T(1,128)S(1)}, s32[1,4]{1,0:T(1,128)}, u32[]{:S(2)}) copy-start(s32[1,4]{1,0:T(1,128)} %param.17) | copy-start | bytes 52
  86.6 15.1 %all-to-all-start.5 = ((f32[8,64,128]{2,1,0:T(8,128)}), f32[8,64,128]{2,1,0:T(8,128)S(1)}, u32[]{:S(2)}, u32[]{:S(2)}) async-start(f32[8,64,128]{2,1,0:T(8,128)} %get-tuple-element.12), calls=%async_computation.5 | async-start | bytes 524288 | tf_op jit(solution)/shard_map/all_to_all | solution.py:29
  101.7 21.6 %all-to-all-start.4 = ((f32[64,1,640]{2,1,0:T(1,128)}), f32[64,1,640]{2,1,0:T(1,128)S(1)}, u32[]{:S(2)}, u32[]{:S(2)}) async-start(f32[64,1,640]{2,1,0:T(1,128)} %copy.12), calls=%async_computation.4 | async-start | bytes 327680 | tf_op jit(solution)/shard_map/all_to_all | solution.py:29
  123.3 15.5 %all-to-all-start.6 = ((f32[64,1,640]{2,1,0:T(1,128)}), f32[64,1,640]{2,1,0:T(1,128)S(1)}, u32[]{:S(2)}, u32[]{:S(2)}) async-start(f32[64,1,640]{2,1,0:T(1,128)} %copy.13), calls=%async_computation.6 | async-start | bytes 327680 | tf_op jit(solution)/shard_map/all_to_all | solution.py:29
  138.8 15.6 %all-to-all-start.3 = ((bf16[64,2,640]{2,1,0:T(2,128)(2,1)}), bf16[64,2,640]{2,1,0:T(2,128)(2,1)S(1)}, u32[]{:S(2)}, u32[]{:S(2)}) async-start(bf16[64,2,640]{2,1,0:T(2,128)(2,1)} %reshape.50), calls=%async_computation.3 | async-start | bytes 327680 | tf_op jit(solution)/shard_map/all_to_all | solution.py:29
  155.3 17.0 %all-to-all-start.7 = ((f32[64,1,1280]{2,1,0:T(1,128)}), f32[64,1,1280]{2,1,0:T(1,128)S(1)}, u32[]{:S(2)}, u32[]{:S(2)}) async-start(f32[64,1,1280]{2,1,0:T(1,128)} %broadcast_in_dim.9), calls=%async_computation.7 | async-start | bytes 655360 | tf_op jit(solution)/shard_map/all_to_all | solution.py:29

commit v2 on v1

v2 whole, which is shorter than its diff:
```python
import functools
import math

import jax
import jax.numpy as jnp
from jax import lax
from jax.experimental import pallas as pl
from jax.experimental.pallas import tpu as pltpu
from jax.sharding import Mesh
from jax.sharding import PartitionSpec as P

HEAD_DIM = 128
REACH = 2
VMEM_BYTES = 48 * 1024 * 1024
START_BYTES = 60 * 1024 * 1024
SEQ = ("pair", "lane")
HEADS_OF = ((0, 1, 2), (3, 4, 2))
UNITS = ((0, 0), (0, 1), (1, 0), (1, 1), (2, None))
NT = (((1,), (1,)), ((), ()))
NN = (((1,), (0,)), ((), ()))
TN = (((0,), (0,)), ((), ()))


def product(left, right, dims=NN):
    return lax.dot_general(left, right, dims, preferred_element_type=jnp.float32)


def shifted(shard, by):
    devices = lax.axis_size("pair")
    return lax.ppermute(shard, "pair", [(i, (i + by) % devices) for i in range(devices)])


def swap(blocks, axis):
    return lax.all_to_all(blocks, axis, split_axis=0, concat_axis=0, tiled=True)


def call(body, out_shape, prefetch=(), operands=(), in_specs=None, vmem=VMEM_BYTES):
    def whole(shape):
        return pl.BlockSpec(shape, lambda i, *_: (0,) * len(shape))

    specs = in_specs or [None] * len(operands)
    return pl.pallas_call(
        body,
        out_shape=out_shape,
        grid_spec=pltpu.PrefetchScalarGridSpec(
            num_scalar_prefetch=len(prefetch),
            grid=(1,),
            in_specs=[s or whole(o.shape) for s, o in zip(specs, operands)],
            out_specs=jax.tree.map(lambda o: whole(o.shape), out_shape),
        ),
        compiler_params=pltpu.CompilerParams(vmem_limit_bytes=vmem),
    )(*prefetch, *operands)


def head(array, index):
    return array[:, index * HEAD_DIM : (index + 1) * HEAD_DIM]


def start_kernel(me, slots, key, value, query_base, grad, hidden, down_t, order, send, part):
    tokens = order.shape[0]
    pairs, lanes, peer, _ = send.shape
    width = key.shape[1]
    part[...] = product(down_t[...], hidden[...], NT)
    target = slots[0] // tokens
    rows = lax.broadcasted_iota(jnp.int32, (tokens, tokens), 0)
    cols = lax.broadcasted_iota(jnp.int32, (tokens, tokens), 1)
    spread = jnp.broadcast_to(target, (tokens, tokens))
    target_col = jnp.sum(jnp.where(rows == cols, spread, 0), axis=1, keepdims=True)
    earlier = jnp.logical_and(target_col == spread, rows < cols)
    rank = jnp.sum(jnp.where(earlier, 1, 0), axis=0, keepdims=True)
    half = pairs * peer
    place = lax.rem(target, lanes) * half + lax.div(target, jnp.int32(lanes)) * peer + rank
    one_hot = jnp.where(rows == place, 1.0, 0.0).astype(jnp.bfloat16)
    order[...] = one_hot

    def by_tile(source):
        moved = product(one_hot, source[...]).astype(jnp.bfloat16)
        return [moved[k * half : (k + 1) * half] for k in range(lanes)]

    def put(lane, start, block):
        send[:, lane, :, start : start + block.shape[1]] = block.reshape(pairs, peer, block.shape[1])

    shared = len(HEADS_OF[0]) * HEAD_DIM
    for k, source in enumerate((key, value)):
        moved = by_tile(source)
        for lane in range(lanes):
            for tile in range(lanes):
                for j, h in enumerate(HEADS_OF[lane]):
                    put(lane, (2 * tile + k) * shared + j * HEAD_DIM, head(moved[tile], h))
    start = 2 * lanes * shared
    for source in (query_base, grad):
        moved = by_tile(source)
        for lane in range(lanes):
            for unit, (j, tile) in enumerate(UNITS):
                put(lane, start + unit * HEAD_DIM, head(moved[lane if tile is None else tile], HEADS_OF[lane][j]))
        start += width


def add_up(parts):
    total = parts[0].astype(jnp.float32)
    for k in range(1, parts.shape[0]):
        total = total + parts[k].astype(jnp.float32)
    return total.astype(jnp.bfloat16)


def second_kernel(parts, hidden, order, send):
    pairs, lanes, peer, _ = send.shape
    half = pairs * peer
    width = hidden.shape[1]
    one_hot = order[...]
    moved = product(one_hot, hidden[...]).astype(jnp.bfloat16)
    low = product(one_hot, add_up(parts), NT).astype(jnp.bfloat16)
    low = jnp.concatenate([low[k * half : (k + 1) * half] for k in range(lanes)], axis=1)
    for lane in range(lanes):
        send[:, lane, :, :width] = moved[lane * half : (lane + 1) * half].reshape(pairs, peer, width)
        send[:, lane, :, width:] = low.reshape(pairs, peer, low.shape[1])


def unpack_kernel(received, after, key_value):
    tokens, width = key_value.shape[0] // 2, key_value.shape[1]
    for tile in range(2):
        key_value[tile * tokens : (tile + 1) * tokens, :] = received[:, :, tile * width : (tile + 1) * width].reshape(
            tokens, width
        )


def query_kernel(first, second, up, lane, query, grad, hidden, low):
    tokens, width = query.shape
    rank = up.shape[0]
    start = first.shape[2] - 2 * width
    low[...] = second[:, :, width:].reshape(tokens, 2 * rank)
    own = lane[0] == 0
    ups = own_heads(up, own)
    low_own = jnp.where(own, low[:, :rank], low[:, rank:])
    for unit, (j, tile) in enumerate(UNITS):
        columns = slice(start + unit * HEAD_DIM, start + (unit + 1) * HEAD_DIM)
        base = first[:, :, columns].reshape(tokens, HEAD_DIM).astype(jnp.float32)
        rows = low_own if tile is None else low[:, tile * rank : (tile + 1) * rank]
        query[:, unit * HEAD_DIM : (unit + 1) * HEAD_DIM] = (base + product(rows, ups[j])).astype(jnp.bfloat16)
    grad[...] = first[:, :, start + width : start + 2 * width].reshape(tokens, width)
    hidden[...] = second[:, :, :width].reshape(tokens, width)


def own_heads(up, own):
    return [jnp.where(own, head(up, a), head(up, b)) for a, b in zip(*HEADS_OF)]


def attend_kernel(
    tiles, lane, window_a, window_b, left, right, centre, queries, grads, low, up, out, low_parts, up_part
):
    tokens = queries.shape[0]
    rank = up.shape[0]
    own = lane[0] == 0
    missing = []
    for tile in range(2):
        total = jnp.int32(0)
        mine = lane[0] == tile
        row = [jnp.where(mine, window_a[k], window_b[k]) for k in range(4)]
        for k in range(1, 4):
            away = lax.rem(row[k] - row[0] + tiles, tiles)
            total = total + jnp.where(away <= REACH, away + REACH, away - (tiles - REACH))
        missing.append(8 - total)
    span = [(array, tile) for array in (left, centre, right) for tile in range(2)]

    def block(index, columns):
        array, tile = span[index]
        return array[tile * tokens : (tile + 1) * tokens, columns]

    def chosen(tile, columns):
        if tile is None:
            skip = jnp.where(own, missing[0], missing[1])
            blocks = []
            for k in range(4):
                near = jnp.where(own, block(k, columns), block(k + 1, columns))
                far = jnp.where(own, block(k + 1, columns), block(k + 2, columns))
                blocks.append(jnp.where(skip <= k, far, near))
            return jnp.concatenate(blocks, axis=0)
        return jnp.concatenate(
            [
                jnp.where(missing[tile] <= k, block(tile + k + 1, columns), block(tile + k, columns))
                for k in range(4)
            ],
            axis=0,
        )

    scale = 1.0 / math.sqrt(HEAD_DIM)
    ups = own_heads(up, own)
    low_own = jnp.where(own, low[:, :rank], low[:, rank:])
    low_of = [jnp.zeros((rank, tokens), jnp.float32) for _ in range(2)]
    up_of = [jnp.zeros((rank, HEAD_DIM), jnp.float32) for _ in ups]
    shared = len(ups) * HEAD_DIM
    for unit, (j, tile) in enumerate(UNITS):
        columns = slice(unit * HEAD_DIM, (unit + 1) * HEAD_DIM)
        keys = chosen(tile, slice(j * HEAD_DIM, (j + 1) * HEAD_DIM))
        values = chosen(tile, slice(shared + j * HEAD_DIM, shared + (j + 1) * HEAD_DIM))
        scores = product(queries[:, columns], keys, NT) * scale
        exps = jnp.exp(scores - jnp.max(scores, axis=-1, keepdims=True))
        weights = exps * (1.0 / jnp.sum(exps, axis=-1, keepdims=True))
        out[:, columns] = product(weights.astype(jnp.bfloat16), values).astype(jnp.bfloat16)
        grad_weights = product(grads[:, columns], values, NT)
        row_dot = jnp.sum(weights * grad_weights, axis=-1, keepdims=True)
        grad_scores = (weights * (grad_weights - row_dot)).astype(jnp.bfloat16)
        grad_query = (product(grad_scores, keys) * scale).astype(jnp.bfloat16)
        low_grad = product(ups[j], grad_query, NT)
        rows = low_own if tile is None else low[:, tile * rank : (tile + 1) * rank]
        up_of[j] = up_of[j] + product(rows, grad_query, TN)
        if tile is None:
            low_of = [
                low_of[0] + jnp.where(own, low_grad, 0.0),
                low_of[1] + jnp.where(own, 0.0, low_grad),
            ]
        else:
            low_of[tile] = low_of[tile] + low_grad
    group = low_parts.shape[0] // 2
    for k in range(low_parts.shape[0]):
        low_parts[k] = low_of[k // group].astype(low_parts.dtype)
    for h in range(up_part.shape[1] // HEAD_DIM):
        halves = [up_of[heads.index(h)] if h in heads else jnp.zeros_like(up_of[0]) for heads in HEADS_OF]
        up_part[:, h * HEAD_DIM : (h + 1) * HEAD_DIM] = jnp.where(own, halves[0], halves[1])


def down_kernel(parts, hidden, out, up_part, send):
    tokens, width = out.shape
    peers, peer, _ = send.shape
    down_part = product(add_up(parts), hidden[...])
    sums = jnp.concatenate([up_part[...], down_part], axis=0).astype(jnp.bfloat16)
    send[:, :, :width] = out[...].reshape(peers, peer, width)
    send[:, :, width:] = sums.reshape(peers, peer, width)


def sum_kernel(received, totals):
    width = totals.shape[2]
    total = jnp.sum(received[:, :, width:].astype(jnp.float32), axis=0, keepdims=True)
    totals[...] = jnp.broadcast_to(total, totals.shape).astype(totals.dtype)


def restore_kernel(order, received, attended):
    tokens, width = attended.shape
    pairs, lanes, peer, _ = received.shape
    tiles = []
    for tile in range(lanes):
        blocks = []
        for h in range(width // HEAD_DIM):
            for lane, heads in enumerate(HEADS_OF):
                for unit, (j, at) in enumerate(UNITS):
                    if heads[j] == h and (lane if at is None else at) == tile:
                        columns = slice(unit * HEAD_DIM, (unit + 1) * HEAD_DIM)
                        blocks.append(received[:, lane, :, columns].reshape(pairs * peer, HEAD_DIM))
        tiles.append(jnp.concatenate(blocks, axis=1))
    attended[...] = product(order[...], jnp.concatenate(tiles, axis=0), TN).astype(jnp.bfloat16)


def split_kernel(totals, up_total, down_total):
    rank, width = up_total.shape
    rows = totals[...].reshape(2 * rank, width).astype(jnp.float32)
    up_total[...] = rows[:rank]
    down_total[...] = rows[rank:]


def local(
    hidden_in,
    query_base,
    key_base,
    value_base,
    grad_out,
    adapter_down,
    adapter_up,
    tile_slot,
    window_table,
):
    tokens, width = hidden_in.shape
    rank = adapter_up.shape[0]
    tiles = lax.axis_size(SEQ)
    lanes = lax.axis_size("lane")
    pairs = tiles // lanes
    group = lax.axis_size("tp")
    peer = tokens // tiles
    shared = len(HEADS_OF[0]) * HEAD_DIM
    bf16, f32 = jnp.bfloat16, jnp.float32
    shape = jax.ShapeDtypeStruct
    me = lax.axis_index(SEQ).astype(jnp.int32).reshape(1)
    lane = lax.axis_index("lane").astype(jnp.int32).reshape(1)
    window = window_table.reshape(-1)
    other_window = lax.ppermute(window, "lane", [(0, 1), (1, 0)])

    columns = 4 * shared + 2 * width
    order, send, low_part = call(
        start_kernel,
        [shape((tokens, tokens), bf16), shape((pairs, lanes, peer, columns), bf16), shape((rank, tokens), f32)],
        (me,),
        (
            tile_slot.reshape(tiles, 1, tokens),
            key_base,
            value_base,
            query_base,
            grad_out,
            hidden_in,
            adapter_down.T,
        ),
        [pl.BlockSpec((1, 1, tokens), lambda i, me: (me[0], 0, 0))] + [None] * 6,
        START_BYTES,
    )
    first = swap(send.reshape(tiles, peer, columns), SEQ)
    low_parts = lax.all_gather(low_part, "tp")
    second_send = call(
        second_kernel,
        shape((pairs, lanes, peer, width + 2 * rank), bf16),
        (),
        (low_parts, hidden_in, order),
    )
    centre = call(
        unpack_kernel,
        shape((2 * tokens, 2 * shared), bf16),
        (),
        (first, second_send),
        [pl.BlockSpec((tiles, peer, 4 * shared), lambda i, *_: (0, 0, 0)), pl.BlockSpec(memory_space=pl.ANY)],
    )
    left, right = shifted(centre, 1), shifted(centre, -1)
    second = swap(second_send.reshape(tiles, peer, width + 2 * rank), SEQ)
    query_tile, grad_tile, hidden_tile, low_tile = call(
        lambda lane, first, second, up, *outs: query_kernel(first, second, up, lane, *outs),
        [shape((tokens, width), bf16)] * 3 + [shape((tokens, 2 * rank), bf16)],
        (lane,),
        (first, second, adapter_up),
    )
    out_tile, low_grad_parts, up_part = call(
        functools.partial(attend_kernel, tiles),
        [shape((tokens, width), bf16), shape((lanes * group, rank, tokens), bf16), shape((rank, width), f32)],
        (lane, window, other_window),
        (left, right, centre, query_tile, grad_tile, low_tile, adapter_up),
    )
    low_grad_parts = swap(low_grad_parts, ("lane", "tp"))
    back_send = call(
        down_kernel,
        shape((tiles, peer, 2 * width), bf16),
        (),
        (low_grad_parts, hidden_tile, out_tile, up_part),
    )
    back = swap(back_send, SEQ)
    totals = swap(call(sum_kernel, shape((tiles, peer, width), bf16), (), (back,)), SEQ)
    attended = call(
        restore_kernel,
        shape((tokens, width), bf16),
        (),
        (order, back.reshape(pairs, lanes, peer, 2 * width)),
    )
    up_total, down_total = call(split_kernel, [shape((rank, width), f32)] * 2, (), (totals,))
    return attended, down_total.T, up_total


def solution(mesh):
    tiles, group = mesh.devices.shape
    lanes = len(HEADS_OF)
    return jax.shard_map(
        local,
        mesh=Mesh(mesh.devices.reshape(tiles // lanes, lanes, group), ("pair", "lane", "tp")),
        in_specs=(
            P(SEQ, "tp"),
            P(SEQ, "tp"),
            P(SEQ, "tp"),
            P(SEQ, "tp"),
            P(SEQ, "tp"),
            P("tp", None),
            P(None, "tp"),
            P(),
            P(SEQ, None),
        ),
        out_specs=(P(SEQ, "tp"), P("tp", None), P(None, "tp")),
        check_vma=False,
    )
```

time: 174 us -> 129 us (0.74)
  waiting for transfers between devices: 84.7 us -> 19.7 us
  blocking collectives: 0 us -> 54.4 us
  starting transfers between devices: 70.9 us -> 41.4 us
  local copies, waits for them, and re-layouts: 8.32 us -> 0.67 us
  Pallas kernels: 8.08 us -> 11.1 us
    all_to_all x8 -> x3, waiting for transfers between devices: 78.3 us -> 19.7 us  [swap(): return lax.all_to_all(blocks, axis, split_axis=0, concat_axis=0, tiled=True)]
    all_to_all x0 -> x2, blocking collectives: none -> 35.2 us  [swap(): return lax.all_to_all(blocks, axis, split_axis=0, concat_axis=0, tiled=True)]
    all_to_all x8 -> x3, starting transfers between devices: 55.2 us -> 30.9 us  [swap(): return lax.all_to_all(blocks, axis, split_axis=0, concat_axis=0, tiled=True)]
    all_gather x0 -> x1, blocking collectives: none -> 19.1 us  [local(): low_parts = lax.all_gather(low_part, 'tp')]
    ppermute x4 -> x3, waiting for transfers between devices: 6.39 us -> 0.01 us  [the longest x2 0.01 us: shifted(): lax.ppermute(shard, 'pair', [(i, (i + by) % devices) for i in range(devic...]
    ppermute x4 -> x3, starting transfers between devices: 15.7 us -> 10.5 us  [the longest x2 8.15 us: shifted(): lax.ppermute(shard, 'pair', [(i, (i + by) % devices) for i in range(devic...]
    reshape x8 -> x0, local copies, waits for them, and re-layouts: 4.81 us -> none  [the longest x2 1.35 us: local(): rows = swap(row_send.reshape(tiles, peer, -1), 'seq').reshape(tokens, -1)]
    pallas_call x6 -> x9, Pallas kernels: 8.08 us -> 11.1 us  [call(): pl.pallas_call(body, out_shape=out_shape, grid_spec=pltpu.PrefetchScalarG...]
  transfers between devices with their start and end apart: 12 -> 6, of which waited for: 11 -> 3; matrix products, arithmetic and copies ran while one was open for 3% -> 0% of each run, Pallas kernels for 1% -> 2%
where the time goes in v2:
time: 129 us; the launch traced here: 128 us
  blocking collectives  54.4 us (42%)
  starting transfers between devices  41.4 us (32%)
  waiting for transfers between devices  19.7 us (15%)
  Pallas kernels  11.1 us (9%)
    all_to_all x2, blocking collectives, swap(): return lax.all_to_all(blocks, axis, split_axis=0, concat_axis=0, tiled=True)  35.2 us
    all_to_all x3, starting transfers between devices, swap(): return lax.all_to_all(blocks, axis, split_axis=0, concat_axis=0, tiled=True)  30.9 us
    all_to_all x3, waiting for transfers between devices, swap(): return lax.all_to_all(blocks, axis, split_axis=0, concat_axis=0, tiled=True)  19.7 us
    all_gather x1, blocking collectives, local(): low_parts = lax.all_gather(low_part, 'tp')  19.1 us
    pallas_call x9, Pallas kernels, call(): pl.pallas_call(body, out_shape=out_shape, grid_spec=pltpu.PrefetchScalarG...  11.1 us
    ppermute x2, starting transfers between devices, shifted(): lax.ppermute(shard, 'pair', [(i, (i + by) % devices) for i in range(devic...  8.15 us
  transfers between devices with their start and end apart: 6, of which 3 were waited for; matrix products, arithmetic and copies ran while one was open for 0% of the time, Pallas kernels for 2%

profile of v2, /device:TPU:8, one launch (start us, length us, event | category | flops | bytes accessed | tf_op | source)
XLA Modules:
  0.0 128.1 jit_solution(18321214549905138903)
XLA Ops:
  0.6 2.9 %shard_map.112 = (bf16[128,128]{1,0:T(8,128)(2,1)}, bf16[32,2,2,2816]{3,2,1,0:T(2,128)(2,1)}, f32[64,128]{1,0:T(8,128)}) custom-call(s32[1]{0:T(128)} %bitcast.me, s32[64,1,128]{2,1,0:T(1,128)} %bitcast.16, bf16[128,640]{1,0:T(8,128)(2,1)} %key.1, bf16[128,640]{1,0:T(8,128)(2,1)} %value.1, bf16[128,640]{1,0:T(8,128)(2,1)} %query_base.1, ...), custom_call_target="tpu_custom_call" | custom-call | tf_op jit(solution)/shard_map/pallas_call | solution.py:42
  3.5 14.9 %all-to-all-start = ((bf16[64,2,2816]{2,1,0:T(2,128)(2,1)}), bf16[64,2,2816]{2,1,0:T(2,128)(2,1)S(1)}, u32[]{:S(2)}, u32[]{:S(2)}) async-start(bf16[64,2,2816]{2,1,0:T(2,128)(2,1)} %bitcast.14), calls=%async_computation | async-start | bytes 1441792 | tf_op jit(solution)/shard_map/all_to_all | solution.py:34
  18.5 0.0 copy-start
  18.5 0.0 copy-done.4
  18.5 0.0 copy-start.2
  18.5 19.1 %all-gather = f32[512,128]{1,0:T(8,128)S(1)} all-gather(f32[64,128]{1,0:T(8,128)S(1)} %copy-done.4), channel_id=2, replica_groups=mesh['pair'=32,'lane'=2,'tp'=8] {'tp'}, dimensions={0}, use_global_device_ids=true | all-gather | bytes 294912 | tf_op jit(solution)/shard_map/all_gather | solution.py:304
  37.7 0.0 copy-done
  37.7 0.0 copy-done.2
  37.7 1.0 shard_map.113.after
  38.6 0.7 all-to-all-done.received.first
  39.4 0.1 shard_map.114.centre
  39.5 6.2 %collective-permute-start.2 = (bf16[256,768]{1,0:T(8,128)(2,1)S(1)}, bf16[256,768]{1,0:T(8,128)(2,1)S(1)}, u32[]{:S(2)}, u32[]{:S(2)}) collective-permute-start(bf16[256,768]{1,0:T(8,128)(2,1)S(1)} %shard_map.114.centre), channel_id=1, source_target_pairs={{0,496},{16,0},{32,16},{48,32},{64,48},{80,64},{96,80},{112,96},{1... | collective-permute-start | bytes 1179656 | tf_op jit(solution)/shard_map/ppermute | solution.py:30
  45.7 1.9 %collective-permute-start.1 = (bf16[256,768]{1,0:T(8,128)(2,1)S(1)}, bf16[256,768]{1,0:T(8,128)(2,1)S(1)}, u32[]{:S(2)}, u32[]{:S(2)}) collective-permute-start(bf16[256,768]{1,0:T(8,128)(2,1)S(1)} %shard_map.114.centre), channel_id=1, source_target_pairs={{0,16},{16,32},{32,48},{48,64},{64,80},{80,96},{96,112},{112,128},... | collective-permute-start | bytes 1179656 | tf_op jit(solution)/shard_map/ppermute | solution.py:30
  47.6 0.0 copy-start.1
  47.6 10.1 %all-to-all-start.1 = ((bf16[64,2,768]{2,1,0:T(2,128)(2,1)}), bf16[64,2,768]{2,1,0:T(2,128)(2,1)S(1)}, u32[]{:S(2)}, u32[]{:S(2)}) async-start(bf16[64,2,768]{2,1,0:T(2,128)(2,1)} %bitcast.7), calls=%async_computation.1 | async-start | bytes 393216 | tf_op jit(solution)/shard_map/all_to_all | solution.py:34
  57.8 0.0 copy-start.3
  57.8 0.6 copy-done.3
  58.4 2.4 %collective-permute-start = (s32[4]{0:T(128)S(1)}, s32[4]{0:T(128)S(1)}, u32[]{:S(2)}, u32[]{:S(2)}) collective-permute-start(s32[4]{0:T(128)S(1)} %bitcast.12), channel_id=1, source_target_pairs={{0,8},{8,0},{1,9},{9,1},{2,10},{10,2},{3,11},{11,3},{4,12},{12,4},... | collective-permute-start | bytes 56 | tf_op jit(solution)/shard_map/ppermute | solution.py:284
  60.8 8.6 %all-to-all-done.1.second = bf16[64,2,768]{2,1,0:T(2,128)(2,1)S(1)} async-done(((bf16[64,2,768]{2,1,0:T(2,128)(2,1)}), bf16[64,2,768]{2,1,0:T(2,128)(2,1)S(1)}, u32[]{:S(2)}, u32[]{:S(2)}) %all-to-all-start.1) | async-done | bytes 196640 | tf_op jit(solution)/shard_map/all_to_all | solution.py:34
  69.4 0.4 shard_map.115
  69.8 0.0 collective-permute-done.window_b
  69.9 0.0 collective-permute-done.2.right
  69.9 0.0 collective-permute-done.1.left
  69.9 4.1 %shard_map.116 = (bf16[128,640]{1,0:T(8,128)(2,1)S(1)}, bf16[16,64,128]{2,1,0:T(8,128)(2,1)S(1)}, f32[64,640]{1,0:T(8,128)S(1)}) custom-call(s32[1]{0:T(128)} %bitcast.3.lane, s32[4]{0:T(128)S(1)} %bitcast.13, s32[4]{0:T(128)S(1)} %collective-permute-done.window_b, bf16[256,768]{1,0:T(8,128)(2,1)S(1)} %collective-permute-done.1.left, ...), custom_call_target="tpu_custom_call" | custom-call | tf_op jit(solution)/shard_map/pallas_call | solution.py:42
  74.0 15.8 %all_to_all.25.parts = bf16[16,64,128]{2,1,0:T(8,128)(2,1)S(1)} all-to-all(bf16[16,64,128]{2,1,0:T(8,128)(2,1)S(1)} %get-tuple-element.21), channel_id=1, replica_groups=mesh['pair'=32,'lane'=2,'tp'=8] {'lane','tp'}, dimensions={0} | all-to-all | bytes 524288 | tf_op jit(solution)/shard_map/all_to_all | solution.py:34
  89.8 0.2 shard_map.117
  90.0 19.4 %all_to_all.26.received = bf16[64,2,1280]{2,1,0:T(2,128)(2,1)S(1)} all-to-all(bf16[64,2,1280]{2,1,0:T(2,128)(2,1)S(1)} %shard_map.117), channel_id=1, replica_groups=mesh['pair'=32,'lane'=2,'tp'=8] {'pair','lane'}, dimensions={0} | all-to-all | bytes 655360 | tf_op jit(solution)/shard_map/all_to_all | solution.py:34
  109.4 0.9 shard_map.119
  110.3 5.8 %all-to-all-start.4 = ((bf16[64,2,640]{2,1,0:T(2,128)(2,1)}), bf16[64,2,640]{2,1,0:T(2,128)(2,1)S(1)}, u32[]{:S(2)}, u32[]{:S(2)}) async-start(bf16[64,2,640]{2,1,0:T(2,128)(2,1)} %shard_map.119), calls=%async_computation.4 | async-start | bytes 327680 | tf_op jit(solution)/shard_map/all_to_all | solution.py:34
  116.1 0.9 shard_map.118
  117.0 10.4 %all-to-all-done.4.totals = bf16[64,2,640]{2,1,0:T(2,128)(2,1)S(1)} async-done(((bf16[64,2,640]{2,1,0:T(2,128)(2,1)}), bf16[64,2,640]{2,1,0:T(2,128)(2,1)S(1)}, u32[]{:S(2)}, u32[]{:S(2)}) %all-to-all-start.4) | async-done | bytes 163872 | tf_op jit(solution)/shard_map/all_to_all | solution.py:34
  127.3 0.8 shard_map.120
  (2 shorter events, 0.0 us)
Async XLA Ops:
  3.5 15.0 %copy-start.4 = (f32[64,128]{1,0:T(8,128)S(1)}, f32[64,128]{1,0:T(8,128)}, u32[]{:S(2)}) copy-start(f32[64,128]{1,0:T(8,128)} %get-tuple-element.17) | copy-start | bytes 98308
  3.5 35.8 %all-to-all-start = ((bf16[64,2,2816]{2,1,0:T(2,128)(2,1)}), bf16[64,2,2816]{2,1,0:T(2,128)(2,1)S(1)}, u32[]{:S(2)}, u32[]{:S(2)}) async-start(bf16[64,2,2816]{2,1,0:T(2,128)(2,1)} %bitcast.14), calls=%async_computation | async-start | bytes 1441792 | tf_op jit(solution)/shard_map/all_to_all | solution.py:34
  18.5 19.2 %copy-start = (bf16[128,640]{1,0:T(8,128)(2,1)S(1)}, bf16[128,640]{1,0:T(8,128)(2,1)}, u32[]{:S(2)}) copy-start(bf16[128,640]{1,0:T(8,128)(2,1)} %hidden.3) | copy-start | bytes 491524
  18.5 19.2 %copy-start.2 = (bf16[128,128]{1,0:T(8,128)(2,1)S(1)}, bf16[128,128]{1,0:T(8,128)(2,1)}, u32[]{:S(2)}) copy-start(bf16[128,128]{1,0:T(8,128)(2,1)} %get-tuple-element.15.order) | copy-start | bytes 98308
  39.5 30.4 %collective-permute-start.2 = (bf16[256,768]{1,0:T(8,128)(2,1)S(1)}, bf16[256,768]{1,0:T(8,128)(2,1)S(1)}, u32[]{:S(2)}, u32[]{:S(2)}) collective-permute-start(bf16[256,768]{1,0:T(8,128)(2,1)S(1)} %shard_map.114.centre), channel_id=1, source_target_pairs={{0,496},{16,0},{32,16},{48,32},{64,48},{80,64},{96,80},{112,96},{1... | collective-permute-start | bytes 1179656 | tf_op jit(solution)/shard_map/ppermute | solution.py:30
  45.7 24.2 %collective-permute-start.1 = (bf16[256,768]{1,0:T(8,128)(2,1)S(1)}, bf16[256,768]{1,0:T(8,128)(2,1)S(1)}, u32[]{:S(2)}, u32[]{:S(2)}) collective-permute-start(bf16[256,768]{1,0:T(8,128)(2,1)S(1)} %shard_map.114.centre), channel_id=1, source_target_pairs={{0,16},{16,32},{32,48},{48,64},{64,80},{80,96},{96,112},{112,128},... | collective-permute-start | bytes 1179656 | tf_op jit(solution)/shard_map/ppermute | solution.py:30
  47.6 21.8 %copy-start.1 = (bf16[64,640]{1,0:T(8,128)(2,1)S(1)}, bf16[64,640]{1,0:T(8,128)(2,1)}, u32[]{:S(2)}) copy-start(bf16[64,640]{1,0:T(8,128)(2,1)} %up.3) | copy-start | bytes 245764
  47.6 21.8 %all-to-all-start.1 = ((bf16[64,2,768]{2,1,0:T(2,128)(2,1)}), bf16[64,2,768]{2,1,0:T(2,128)(2,1)S(1)}, u32[]{:S(2)}, u32[]{:S(2)}) async-start(bf16[64,2,768]{2,1,0:T(2,128)(2,1)} %bitcast.7), calls=%async_computation.1 | async-start | bytes 393216 | tf_op jit(solution)/shard_map/all_to_all | solution.py:34
  57.8 0.7 copy-start.3
  58.4 11.4 %collective-permute-start = (s32[4]{0:T(128)S(1)}, s32[4]{0:T(128)S(1)}, u32[]{:S(2)}, u32[]{:S(2)}) collective-permute-start(s32[4]{0:T(128)S(1)} %bitcast.12), channel_id=1, source_target_pairs={{0,8},{8,0},{1,9},{9,1},{2,10},{10,2},{3,11},{11,3},{4,12},{12,4},... | collective-permute-start | bytes 56 | tf_op jit(solution)/shard_map/ppermute | solution.py:284
  110.3 17.1 %all-to-all-start.4 = ((bf16[64,2,640]{2,1,0:T(2,128)(2,1)}), bf16[64,2,640]{2,1,0:T(2,128)(2,1)S(1)}, u32[]{:S(2)}, u32[]{:S(2)}) async-start(bf16[64,2,640]{2,1,0:T(2,128)(2,1)} %shard_map.119), calls=%async_computation.4 | async-start | bytes 327680 | tf_op jit(solution)/shard_map/all_to_all | solution.py:34

commit v3 on v2

--- a/solution.py
+++ b/solution.py
@@ -11,6 +11,8 @@
 
 HEAD_DIM = 128
 REACH = 2
+FIRST = ('base', 'grad')
+SECOND = ('hidden',)
 VMEM_BYTES = 48 * 1024 * 1024
 START_BYTES = 60 * 1024 * 1024
 SEQ = ("pair", "lane")
@@ -56,11 +58,21 @@
     return array[:, index * HEAD_DIM : (index + 1) * HEAD_DIM]
 
 
-def start_kernel(me, slots, key, value, query_base, grad, hidden, down_t, order, send, part):
+def place_rows(name, moved, put, start, lanes):
+    for lane in range(lanes):
+        if name == "hidden":
+            put(lane, start, moved[lane])
+        else:
+            for unit, (j, tile) in enumerate(UNITS):
+                put(lane, start + unit * HEAD_DIM, head(moved[lane if tile is None else tile], HEADS_OF[lane][j]))
+
+
+def start_kernel(tiles, me, slots, window, key, value, hidden, down_t, *refs):
+    *others, order, send, part = refs
     tokens = order.shape[0]
     pairs, lanes, peer, _ = send.shape
     width = key.shape[1]
-    part[...] = product(down_t[...], hidden[...], NT)
+    part[...] = product(down_t[...], hidden[...], NT).astype(part.dtype)
     target = slots[0] // tokens
     rows = lax.broadcasted_iota(jnp.int32, (tokens, tokens), 0)
     cols = lax.broadcasted_iota(jnp.int32, (tokens, tokens), 1)
@@ -88,12 +100,15 @@
                 for j, h in enumerate(HEADS_OF[lane]):
                     put(lane, (2 * tile + k) * shared + j * HEAD_DIM, head(moved[tile], h))
     start = 2 * lanes * shared
-    for source in (query_base, grad):
-        moved = by_tile(source)
-        for lane in range(lanes):
-            for unit, (j, tile) in enumerate(UNITS):
-                put(lane, start + unit * HEAD_DIM, head(moved[lane if tile is None else tile], HEADS_OF[lane][j]))
+    for name, source in zip(FIRST, others):
+        place_rows(name, by_tile(source), put, start, lanes)
         start += width
+    away = lax.rem(window[...] - me[0] + tiles, tiles)
+    listed = jnp.where(away <= REACH, away + REACH, away - (tiles - REACH))
+    missing = 5 * REACH - jnp.sum(listed, axis=1, keepdims=True)
+    noted = jnp.broadcast_to(missing.astype(jnp.float32), (half, HEAD_DIM)).astype(jnp.bfloat16)
+    for lane in range(lanes):
+        put(lane, start, noted)
 
 
 def add_up(parts):
@@ -103,17 +118,26 @@
     return total.astype(jnp.bfloat16)
 
 
-def second_kernel(parts, hidden, order, send):
+def second_kernel(parts, order, *refs):
+    *others, send = refs
     pairs, lanes, peer, _ = send.shape
     half = pairs * peer
-    width = hidden.shape[1]
     one_hot = order[...]
-    moved = product(one_hot, hidden[...]).astype(jnp.bfloat16)
-    low = product(one_hot, add_up(parts), NT).astype(jnp.bfloat16)
-    low = jnp.concatenate([low[k * half : (k + 1) * half] for k in range(lanes)], axis=1)
+
+    def by_tile(product_of):
+        moved = product_of.astype(jnp.bfloat16)
+        return [moved[k * half : (k + 1) * half] for k in range(lanes)]
+
+    def put(lane, start, block):
+        send[:, lane, :, start : start + block.shape[1]] = block.reshape(pairs, peer, block.shape[1])
+
+    start = 0
+    for name, source in zip(SECOND, others):
+        place_rows(name, by_tile(product(one_hot, source[...])), put, start, lanes)
+        start += source.shape[1]
+    low = jnp.concatenate(by_tile(product(one_hot, add_up(parts), NT)), axis=1)
     for lane in range(lanes):
-        send[:, lane, :, :width] = moved[lane * half : (lane + 1) * half].reshape(pairs, peer, width)
-        send[:, lane, :, width:] = low.reshape(pairs, peer, low.shape[1])
+        put(lane, start, low)
 
 
 def unpack_kernel(received, after, key_value):
@@ -124,42 +148,24 @@
         )
 
 
-def query_kernel(first, second, up, lane, query, grad, hidden, low):
-    tokens, width = query.shape
-    rank = up.shape[0]
-    start = first.shape[2] - 2 * width
-    low[...] = second[:, :, width:].reshape(tokens, 2 * rank)
-    own = lane[0] == 0
-    ups = own_heads(up, own)
-    low_own = jnp.where(own, low[:, :rank], low[:, rank:])
-    for unit, (j, tile) in enumerate(UNITS):
-        columns = slice(start + unit * HEAD_DIM, start + (unit + 1) * HEAD_DIM)
-        base = first[:, :, columns].reshape(tokens, HEAD_DIM).astype(jnp.float32)
-        rows = low_own if tile is None else low[:, tile * rank : (tile + 1) * rank]
-        query[:, unit * HEAD_DIM : (unit + 1) * HEAD_DIM] = (base + product(rows, ups[j])).astype(jnp.bfloat16)
-    grad[...] = first[:, :, start + width : start + 2 * width].reshape(tokens, width)
-    hidden[...] = second[:, :, :width].reshape(tokens, width)
-
-
 def own_heads(up, own):
     return [jnp.where(own, head(up, a), head(up, b)) for a, b in zip(*HEADS_OF)]
 
 
-def attend_kernel(
-    tiles, lane, window_a, window_b, left, right, centre, queries, grads, low, up, out, low_parts, up_part
-):
-    tokens = queries.shape[0]
+def attend_kernel(me, left, right, centre, first, second, up, out, low_parts, up_part):
+    tokens, width = out.shape
     rank = up.shape[0]
-    own = lane[0] == 0
-    missing = []
-    for tile in range(2):
-        total = jnp.int32(0)
-        mine = lane[0] == tile
-        row = [jnp.where(mine, window_a[k], window_b[k]) for k in range(4)]
-        for k in range(1, 4):
-            away = lax.rem(row[k] - row[0] + tiles, tiles)
-            total = total + jnp.where(away <= REACH, away + REACH, away - (tiles - REACH))
-        missing.append(8 - total)
+    lane = lax.rem(me[0], 2)
+    own = lane == 0
+    low_start = second.shape[2] - 2 * rank
+    low = second[:, :, low_start : low_start + 2 * rank].reshape(tokens, 2 * rank)
+    noted = [first[pl.ds(me[0] - lane + tile, 1), :, first.shape[2] - HEAD_DIM :] for tile in range(2)]
+    missing = [jnp.max(note.astype(jnp.float32)).astype(jnp.int32) for note in noted]
+
+    def unit_of(name, at):
+        start = first.shape[2] - HEAD_DIM - (len(FIRST) - FIRST.index(name)) * width
+        return first[:, :, start + at.start : start + at.stop].reshape(tokens, HEAD_DIM)
+
     span = [(array, tile) for array in (left, centre, right) for tile in range(2)]
 
     def block(index, columns):
@@ -189,20 +195,28 @@
     low_of = [jnp.zeros((rank, tokens), jnp.float32) for _ in range(2)]
     up_of = [jnp.zeros((rank, HEAD_DIM), jnp.float32) for _ in ups]
     shared = len(ups) * HEAD_DIM
-    for unit, (j, tile) in enumerate(UNITS):
-        columns = slice(unit * HEAD_DIM, (unit + 1) * HEAD_DIM)
-        keys = chosen(tile, slice(j * HEAD_DIM, (j + 1) * HEAD_DIM))
-        values = chosen(tile, slice(shared + j * HEAD_DIM, shared + (j + 1) * HEAD_DIM))
-        scores = product(queries[:, columns], keys, NT) * scale
-        exps = jnp.exp(scores - jnp.max(scores, axis=-1, keepdims=True))
-        weights = exps * (1.0 / jnp.sum(exps, axis=-1, keepdims=True))
-        out[:, columns] = product(weights.astype(jnp.bfloat16), values).astype(jnp.bfloat16)
-        grad_weights = product(grads[:, columns], values, NT)
-        row_dot = jnp.sum(weights * grad_weights, axis=-1, keepdims=True)
-        grad_scores = (weights * (grad_weights - row_dot)).astype(jnp.bfloat16)
-        grad_query = (product(grad_scores, keys) * scale).astype(jnp.bfloat16)
+    places = [slice(unit * HEAD_DIM, (unit + 1) * HEAD_DIM) for unit in range(len(UNITS))]
+    keys = [chosen(tile, slice(j * HEAD_DIM, (j + 1) * HEAD_DIM)) for j, tile in UNITS]
+    values = [chosen(tile, slice(shared + j * HEAD_DIM, shared + (j + 1) * HEAD_DIM)) for j, tile in UNITS]
+    lows = [low_own if tile is None else low[:, tile * rank : (tile + 1) * rank] for _, tile in UNITS]
+    queries = [
+        (unit_of("base", at).astype(jnp.float32) + product(rows, ups[j])).astype(jnp.bfloat16)
+        for at, rows, (j, _) in zip(places, lows, UNITS)
+    ]
+    scores = [product(query, k, NT) * scale for query, k in zip(queries, keys)]
+    grad_weights = [product(unit_of("grad", at), v, NT) for at, v in zip(places, values)]
+    weights, grad_scores = [], []
+    for score, grad_weight in zip(scores, grad_weights):
+        exps = jnp.exp(score - jnp.max(score, axis=-1, keepdims=True))
+        weight = exps * (1.0 / jnp.sum(exps, axis=-1, keepdims=True))
+        row_dot = jnp.sum(weight * grad_weight, axis=-1, keepdims=True)
+        grad_scores.append((weight * (grad_weight - row_dot)).astype(jnp.bfloat16))
+        weights.append(weight.astype(jnp.bfloat16))
+    for at, weight, value in zip(places, weights, values):
+        out[:, at] = product(weight, value).astype(jnp.bfloat16)
+    grad_queries = [(product(g, k) * scale).astype(jnp.bfloat16) for g, k in zip(grad_scores, keys)]
+    for (j, tile), rows, grad_query in zip(UNITS, lows, grad_queries):
         low_grad = product(ups[j], grad_query, NT)
-        rows = low_own if tile is None else low[:, tile * rank : (tile + 1) * rank]
         up_of[j] = up_of[j] + product(rows, grad_query, TN)
         if tile is None:
             low_of = [
@@ -219,19 +233,24 @@
         up_part[:, h * HEAD_DIM : (h + 1) * HEAD_DIM] = jnp.where(own, halves[0], halves[1])
 
 
-def down_kernel(parts, hidden, out, up_part, send):
+def down_kernel(parts, second, out, up_part, send):
     tokens, width = out.shape
     peers, peer, _ = send.shape
-    down_part = product(add_up(parts), hidden[...])
+    start = SECOND.index("hidden") * width
+    down_part = product(add_up(parts), second[:, :, start : start + width].reshape(tokens, width))
     sums = jnp.concatenate([up_part[...], down_part], axis=0).astype(jnp.bfloat16)
     send[:, :, :width] = out[...].reshape(peers, peer, width)
     send[:, :, width:] = sums.reshape(peers, peer, width)
 
 
 def sum_kernel(received, totals):
-    width = totals.shape[2]
-    total = jnp.sum(received[:, :, width:].astype(jnp.float32), axis=0, keepdims=True)
-    totals[...] = jnp.broadcast_to(total, totals.shape).astype(totals.dtype)
+    peers, peer, width = totals.shape
+    count = peers * peer
+    rows = lax.broadcasted_iota(jnp.int32, (count, count), 0)
+    cols = lax.broadcasted_iota(jnp.int32, (count, count), 1)
+    same = jnp.where(lax.rem(rows, peer) == lax.rem(cols, peer), 1.0, 0.0).astype(jnp.bfloat16)
+    total = product(same, received[:, :, width:].reshape(count, width))
+    totals[...] = total.astype(totals.dtype).reshape(peers, peer, width)
 
 
 def restore_kernel(order, received, attended):
@@ -279,34 +298,37 @@
     bf16, f32 = jnp.bfloat16, jnp.float32
     shape = jax.ShapeDtypeStruct
     me = lax.axis_index(SEQ).astype(jnp.int32).reshape(1)
-    lane = lax.axis_index("lane").astype(jnp.int32).reshape(1)
-    window = window_table.reshape(-1)
-    other_window = lax.ppermute(window, "lane", [(0, 1), (1, 0)])
-
-    columns = 4 * shared + 2 * width
+
+    columns = 4 * shared + len(FIRST) * width + HEAD_DIM
+    named = {"base": query_base, "grad": grad_out, "hidden": hidden_in}
     order, send, low_part = call(
-        start_kernel,
-        [shape((tokens, tokens), bf16), shape((pairs, lanes, peer, columns), bf16), shape((rank, tokens), f32)],
+        functools.partial(start_kernel, tiles),
+        [
+            shape((tokens, tokens), bf16),
+            shape((pairs, lanes, peer, columns), bf16),
+            shape((rank, tokens), f32),
+        ],
         (me,),
         (
             tile_slot.reshape(tiles, 1, tokens),
+            window_table,
             key_base,
             value_base,
-            query_base,
-            grad_out,
             hidden_in,
             adapter_down.T,
+            *(named[name] for name in FIRST if name != "hidden"),
         ),
-        [pl.BlockSpec((1, 1, tokens), lambda i, me: (me[0], 0, 0))] + [None] * 6,
+        [pl.BlockSpec((1, 1, tokens), lambda i, me: (me[0], 0, 0))] + [None] * (5 + len(FIRST) - ("hidden" in FIRST)),
         START_BYTES,
     )
     first = swap(send.reshape(tiles, peer, columns), SEQ)
     low_parts = lax.all_gather(low_part, "tp")
+    second_width = len(SECOND) * width + 2 * rank
     second_send = call(
         second_kernel,
-        shape((pairs, lanes, peer, width + 2 * rank), bf16),
+        shape((pairs, lanes, peer, second_width), bf16),
         (),
-        (low_parts, hidden_in, order),
+        (low_parts, order, *(named[name] for name in SECOND)),
     )
     centre = call(
         unpack_kernel,
@@ -316,25 +338,19 @@
         [pl.BlockSpec((tiles, peer, 4 * shared), lambda i, *_: (0, 0, 0)), pl.BlockSpec(memory_space=pl.ANY)],
     )
     left, right = shifted(centre, 1), shifted(centre, -1)
-    second = swap(second_send.reshape(tiles, peer, width + 2 * rank), SEQ)
-    query_tile, grad_tile, hidden_tile, low_tile = call(
-        lambda lane, first, second, up, *outs: query_kernel(first, second, up, lane, *outs),
-        [shape((tokens, width), bf16)] * 3 + [shape((tokens, 2 * rank), bf16)],
-        (lane,),
-        (first, second, adapter_up),
-    )
+    second = swap(second_send.reshape(tiles, peer, second_width), SEQ)
     out_tile, low_grad_parts, up_part = call(
-        functools.partial(attend_kernel, tiles),
+        attend_kernel,
         [shape((tokens, width), bf16), shape((lanes * group, rank, tokens), bf16), shape((rank, width), f32)],
-        (lane, window, other_window),
-        (left, right, centre, query_tile, grad_tile, low_tile, adapter_up),
+        (me,),
+        (left, right, centre, first, second, adapter_up),
     )
     low_grad_parts = swap(low_grad_parts, ("lane", "tp"))
     back_send = call(
         down_kernel,
         shape((tiles, peer, 2 * width), bf16),
         (),
-        (low_grad_parts, hidden_tile, out_tile, up_part),
+        (low_grad_parts, second, out_tile, up_part),
     )
     back = swap(back_send, SEQ)
     totals = swap(call(sum_kernel, shape((tiles, peer, width), bf16), (), (back,)), SEQ)

time: 129 us -> 126 us (0.977)
  blocking collectives: 54.4 us -> 76.3 us
  starting transfers between devices: 41.4 us -> 27.9 us
  waiting for transfers between devices: 19.7 us -> 12.1 us
  Pallas kernels: 11.1 us -> 7.85 us
    all_to_all x2 -> x3, blocking collectives: 35.2 us -> 56.8 us  [swap(): return lax.all_to_all(blocks, axis, split_axis=0, concat_axis=0, tiled=True)]
    all_to_all x3 -> x2, starting transfers between devices: 30.9 us -> 20.8 us  [swap(): return lax.all_to_all(blocks, axis, split_axis=0, concat_axis=0, tiled=True)]
    all_to_all x3 -> x2, waiting for transfers between devices: 19.7 us -> 12.1 us  [swap(): return lax.all_to_all(blocks, axis, split_axis=0, concat_axis=0, tiled=True)]
    pallas_call x9 -> x8, Pallas kernels: 11.1 us -> 7.85 us  [call(): pl.pallas_call(body, out_shape=out_shape, grid_spec=pltpu.PrefetchScalarG...]
    ppermute x1 -> x0, starting transfers between devices: 2.35 us -> none  [local(): other_window = lax.ppermute(window, 'lane', [(0, 1), (1, 0)])]
  transfers between devices with their start and end apart: 6 -> 4, of which waited for: 3 -> 2; matrix products, arithmetic and copies ran while one was open for 0% -> 0% of each run, Pallas kernels for 2% -> 1%
where the time goes in v3:
time: 126 us; the launch traced here: 125 us
  blocking collectives  76.3 us (61%)
  starting transfers between devices  27.9 us (22%)
  waiting for transfers between devices  12.1 us (10%)
  Pallas kernels  7.85 us (6%)
    all_to_all x3, blocking collectives, swap(): return lax.all_to_all(blocks, axis, split_axis=0, concat_axis=0, tiled=True)  56.8 us
    all_to_all x2, starting transfers between devices, swap(): return lax.all_to_all(blocks, axis, split_axis=0, concat_axis=0, tiled=True)  20.8 us
    all_gather x1, blocking collectives, local(): low_parts = lax.all_gather(low_part, 'tp')  19.5 us
    all_to_all x2, waiting for transfers between devices, swap(): return lax.all_to_all(blocks, axis, split_axis=0, concat_axis=0, tiled=True)  12.1 us
    pallas_call x8, Pallas kernels, call(): pl.pallas_call(body, out_shape=out_shape, grid_spec=pltpu.PrefetchScalarG...  7.85 us
    ppermute x2, starting transfers between devices, shifted(): lax.ppermute(shard, 'pair', [(i, (i + by) % devices) for i in range(devic...  7.14 us
  transfers between devices with their start and end apart: 4, of which 2 were waited for; matrix products, arithmetic and copies ran while one was open for 0% of the time, Pallas kernels for 1%

profile of v3, /device:TPU:8, one launch (start us, length us, event | category | flops | bytes accessed | tf_op | source)
XLA Modules:
  0.0 125.0 jit_solution(6602729140466833451)
XLA Ops:
  0.6 2.9 %shard_map.112 = (bf16[128,128]{1,0:T(8,128)(2,1)}, bf16[32,2,2,2944]{3,2,1,0:T(2,128)(2,1)}, f32[64,128]{1,0:T(8,128)}) custom-call(s32[1]{0:T(128)} %bitcast.me, s32[64,1,128]{2,1,0:T(1,128)} %bitcast.13, s32[1,4]{1,0:T(1,128)} %window.1, bf16[128,640]{1,0:T(8,128)(2,1)} %key.1, bf16[128,640]{1,0:T(8,128)(2,1)} %value.1, bf16[128,640]{1,0:T(8,128)(2,1)} %refs_0_.3, ...), custom_call_target="tpu_custom_call" | custom-call | tf_op jit(solution)/shard_map/pallas_call | solution.py:44
  3.5 0.0 copy-start.3
  3.5 14.9 %all-to-all-start = ((bf16[64,2,2944]{2,1,0:T(2,128)(2,1)}), bf16[64,2,2944]{2,1,0:T(2,128)(2,1)S(1)}, u32[]{:S(2)}, u32[]{:S(2)}) async-start(bf16[64,2,2944]{2,1,0:T(2,128)(2,1)} %bitcast.11), calls=%async_computation | async-start | bytes 1507328 | tf_op jit(solution)/shard_map/all_to_all | solution.py:36
  18.5 0.0 copy-start
  18.5 0.0 copy-done.3
  18.5 0.0 copy-start.1
  18.5 19.5 %all-gather = f32[512,128]{1,0:T(8,128)S(1)} all-gather(f32[64,128]{1,0:T(8,128)S(1)} %copy-done.3), channel_id=2, replica_groups=mesh['pair'=32,'lane'=2,'tp'=8] {'tp'}, dimensions={0}, use_global_device_ids=true | all-gather | bytes 294912 | tf_op jit(solution)/shard_map/all_gather | solution.py:325
  38.0 0.0 copy-done
  38.0 0.0 copy-done.1
  38.0 0.3 shard_map.113.after
  38.3 1.7 %all-to-all-done.received.first = bf16[64,2,2944]{2,1,0:T(2,128)(2,1)S(1)} async-done(((bf16[64,2,2944]{2,1,0:T(2,128)(2,1)}), bf16[64,2,2944]{2,1,0:T(2,128)(2,1)S(1)}, u32[]{:S(2)}, u32[]{:S(2)}) %all-to-all-start) | async-done | bytes 753696 | tf_op jit(solution)/shard_map/all_to_all | solution.py:36
  40.1 0.1 shard_map.114.centre
  40.2 5.2 %collective-permute-start.1 = (bf16[256,768]{1,0:T(8,128)(2,1)S(1)}, bf16[256,768]{1,0:T(8,128)(2,1)S(1)}, u32[]{:S(2)}, u32[]{:S(2)}) collective-permute-start(bf16[256,768]{1,0:T(8,128)(2,1)S(1)} %shard_map.114.centre), channel_id=1, source_target_pairs={{0,496},{16,0},{32,16},{48,32},{64,48},{80,64},{96,80},{112,96},{1... | collective-permute-start | bytes 1179656 | tf_op jit(solution)/shard_map/ppermute | solution.py:32
  45.4 1.9 %collective-permute-start = (bf16[256,768]{1,0:T(8,128)(2,1)S(1)}, bf16[256,768]{1,0:T(8,128)(2,1)S(1)}, u32[]{:S(2)}, u32[]{:S(2)}) collective-permute-start(bf16[256,768]{1,0:T(8,128)(2,1)S(1)} %shard_map.114.centre), channel_id=1, source_target_pairs={{0,16},{16,32},{32,48},{48,64},{64,80},{80,96},{96,112},{112,128},... | collective-permute-start | bytes 1179656 | tf_op jit(solution)/shard_map/ppermute | solution.py:32
  47.3 0.0 copy-start.2
  47.3 21.5 %all_to_all.25.second = bf16[64,2,768]{2,1,0:T(2,128)(2,1)S(1)} all-to-all(bf16[64,2,768]{2,1,0:T(2,128)(2,1)S(1)} %bitcast.9), channel_id=1, replica_groups=mesh['pair'=32,'lane'=2,'tp'=8] {'pair','lane'}, dimensions={0} | all-to-all | bytes 393216 | tf_op jit(solution)/shard_map/all_to_all | solution.py:36
  68.9 0.0 collective-permute-done.1.right
  68.9 0.0 collective-permute-done.left
  68.9 0.0 copy-done.2
  68.9 1.8 %shard_map.115 = (bf16[128,640]{1,0:T(8,128)(2,1)S(1)}, bf16[16,64,128]{2,1,0:T(8,128)(2,1)S(1)}, f32[64,640]{1,0:T(8,128)S(1)}) custom-call(s32[1]{0:T(128)} %bitcast.me, bf16[256,768]{1,0:T(8,128)(2,1)S(1)} %collective-permute-done.left, bf16[256,768]{1,0:T(8,128)(2,1)S(1)} %collective-permute-done.1.right, bf16[256,768]{1,0:T(8,128)(2,1)S(1)} %shard_map.114.centre, ...), custom_call_target="tpu_custom_call" | custom-call | tf_op jit(solution)/shard_map/pallas_call | solution.py:44
  70.8 15.9 %all_to_all.26.parts = bf16[16,64,128]{2,1,0:T(8,128)(2,1)S(1)} all-to-all(bf16[16,64,128]{2,1,0:T(8,128)(2,1)S(1)} %get-tuple-element.14), channel_id=1, replica_groups=mesh['pair'=32,'lane'=2,'tp'=8] {'lane','tp'}, dimensions={0} | all-to-all | bytes 524288 | tf_op jit(solution)/shard_map/all_to_all | solution.py:36
  86.7 0.2 shard_map.116
  86.9 19.4 %all_to_all.27.received = bf16[64,2,1280]{2,1,0:T(2,128)(2,1)S(1)} all-to-all(bf16[64,2,1280]{2,1,0:T(2,128)(2,1)S(1)} %shard_map.116), channel_id=1, replica_groups=mesh['pair'=32,'lane'=2,'tp'=8] {'pair','lane'}, dimensions={0} | all-to-all | bytes 655360 | tf_op jit(solution)/shard_map/all_to_all | solution.py:36
  106.2 0.9 shard_map.118
  107.1 5.9 %all-to-all-start.4 = ((bf16[64,2,640]{2,1,0:T(2,128)(2,1)}), bf16[64,2,640]{2,1,0:T(2,128)(2,1)S(1)}, u32[]{:S(2)}, u32[]{:S(2)}) async-start(bf16[64,2,640]{2,1,0:T(2,128)(2,1)} %shard_map.118), calls=%async_computation.4 | async-start | bytes 327680 | tf_op jit(solution)/shard_map/all_to_all | solution.py:36
  113.0 0.9 shard_map.117
  113.9 10.4 %all-to-all-done.4.totals = bf16[64,2,640]{2,1,0:T(2,128)(2,1)S(1)} async-done(((bf16[64,2,640]{2,1,0:T(2,128)(2,1)}), bf16[64,2,640]{2,1,0:T(2,128)(2,1)S(1)}, u32[]{:S(2)}, u32[]{:S(2)}) %all-to-all-start.4) | async-done | bytes 163872 | tf_op jit(solution)/shard_map/all_to_all | solution.py:36
  124.3 0.8 shard_map.119
Async XLA Ops:
  3.5 15.0 %copy-start.3 = (f32[64,128]{1,0:T(8,128)S(1)}, f32[64,128]{1,0:T(8,128)}, u32[]{:S(2)}) copy-start(f32[64,128]{1,0:T(8,128)} %get-tuple-element.13) | copy-start | bytes 98308
  3.5 36.5 %all-to-all-start = ((bf16[64,2,2944]{2,1,0:T(2,128)(2,1)}), bf16[64,2,2944]{2,1,0:T(2,128)(2,1)S(1)}, u32[]{:S(2)}, u32[]{:S(2)}) async-start(bf16[64,2,2944]{2,1,0:T(2,128)(2,1)} %bitcast.11), calls=%async_computation | async-start | bytes 1507328 | tf_op jit(solution)/shard_map/all_to_all | solution.py:36
  18.5 19.6 %copy-start = (bf16[128,640]{1,0:T(8,128)(2,1)S(1)}, bf16[128,640]{1,0:T(8,128)(2,1)}, u32[]{:S(2)}) copy-start(bf16[128,640]{1,0:T(8,128)(2,1)} %refs_0_.3) | copy-start | bytes 491524
  18.5 19.5 %copy-start.1 = (bf16[128,128]{1,0:T(8,128)(2,1)S(1)}, bf16[128,128]{1,0:T(8,128)(2,1)}, u32[]{:S(2)}) copy-start(bf16[128,128]{1,0:T(8,128)(2,1)} %get-tuple-element.11.order) | copy-start | bytes 98308
  40.2 28.7 %collective-permute-start.1 = (bf16[256,768]{1,0:T(8,128)(2,1)S(1)}, bf16[256,768]{1,0:T(8,128)(2,1)S(1)}, u32[]{:S(2)}, u32[]{:S(2)}) collective-permute-start(bf16[256,768]{1,0:T(8,128)(2,1)S(1)} %shard_map.114.centre), channel_id=1, source_target_pairs={{0,496},{16,0},{32,16},{48,32},{64,48},{80,64},{96,80},{112,96},{1... | collective-permute-start | bytes 1179656 | tf_op jit(solution)/shard_map/ppermute | solution.py:32
  45.4 23.5 %collective-permute-start = (bf16[256,768]{1,0:T(8,128)(2,1)S(1)}, bf16[256,768]{1,0:T(8,128)(2,1)S(1)}, u32[]{:S(2)}, u32[]{:S(2)}) collective-permute-start(bf16[256,768]{1,0:T(8,128)(2,1)S(1)} %shard_map.114.centre), channel_id=1, source_target_pairs={{0,16},{16,32},{32,48},{48,64},{64,80},{80,96},{96,112},{112,128},... | collective-permute-start | bytes 1179656 | tf_op jit(solution)/shard_map/ppermute | solution.py:32
  47.3 21.6 %copy-start.2 = (bf16[64,640]{1,0:T(8,128)(2,1)S(1)}, bf16[64,640]{1,0:T(8,128)(2,1)}, u32[]{:S(2)}) copy-start(bf16[64,640]{1,0:T(8,128)(2,1)} %up.1) | copy-start | bytes 245764
  107.1 17.2 %all-to-all-start.4 = ((bf16[64,2,640]{2,1,0:T(2,128)(2,1)}), bf16[64,2,640]{2,1,0:T(2,128)(2,1)S(1)}, u32[]{:S(2)}, u32[]{:S(2)}) async-start(bf16[64,2,640]{2,1,0:T(2,128)(2,1)} %shard_map.118), calls=%async_computation.4 | async-start | bytes 327680 | tf_op jit(solution)/shard_map/all_to_all | solution.py:36

commit v4 on v3

--- a/solution.py
+++ b/solution.py
@@ -253,7 +253,8 @@
     totals[...] = total.astype(totals.dtype).reshape(peers, peer, width)
 
 
-def restore_kernel(order, received, attended):
+def finish_kernel(order, received, totals, attended, up_total, down_total):
+    rank = up_total.shape[0]
     tokens, width = attended.shape
     pairs, lanes, peer, _ = received.shape
     tiles = []
@@ -267,13 +268,9 @@
                         blocks.append(received[:, lane, :, columns].reshape(pairs * peer, HEAD_DIM))
         tiles.append(jnp.concatenate(blocks, axis=1))
     attended[...] = product(order[...], jnp.concatenate(tiles, axis=0), TN).astype(jnp.bfloat16)
-
-
-def split_kernel(totals, up_total, down_total):
-    rank, width = up_total.shape
-    rows = totals[...].reshape(2 * rank, width).astype(jnp.float32)
-    up_total[...] = rows[:rank]
-    down_total[...] = rows[rank:]
+    sums = totals[...].reshape(2 * rank, width).astype(jnp.float32)
+    up_total[...] = sums[:rank]
+    down_total[...] = sums[rank:]
 
 
 def local(
@@ -354,13 +351,12 @@
     )
     back = swap(back_send, SEQ)
     totals = swap(call(sum_kernel, shape((tiles, peer, width), bf16), (), (back,)), SEQ)
-    attended = call(
-        restore_kernel,
-        shape((tokens, width), bf16),
+    attended, up_total, down_total = call(
+        finish_kernel,
+        [shape((tokens, width), bf16)] + [shape((rank, width), f32)] * 2,
         (),
-        (order, back.reshape(pairs, lanes, peer, 2 * width)),
-    )
-    up_total, down_total = call(split_kernel, [shape((rank, width), f32)] * 2, (), (totals,))
+        (order, back.reshape(pairs, lanes, peer, 2 * width), totals),
+    )
     return attended, down_total.T, up_total
 
 

time: 126 us -> 125 us (level)
  blocking collectives: 76.3 us -> 93.3 us
  waiting for transfers between devices: 12.1 us -> 1.75 us
  starting transfers between devices: 27.9 us -> 22.1 us
  Pallas kernels: 7.85 us -> 6.48 us
    all_to_all x3 -> x4, blocking collectives: 56.8 us -> 73.8 us  [swap(): return lax.all_to_all(blocks, axis, split_axis=0, concat_axis=0, tiled=True)]
    all_to_all x2 -> x1, waiting for transfers between devices: 12.1 us -> 1.75 us  [swap(): return lax.all_to_all(blocks, axis, split_axis=0, concat_axis=0, tiled=True)]
    all_to_all x2 -> x1, starting transfers between devices: 20.8 us -> 14.9 us  [swap(): return lax.all_to_all(blocks, axis, split_axis=0, concat_axis=0, tiled=True)]
    pallas_call x8 -> x7, Pallas kernels: 7.85 us -> 6.48 us  [call(): pl.pallas_call(body, out_shape=out_shape, grid_spec=pltpu.PrefetchScalarG...]
  transfers between devices with their start and end apart: 4 -> 3, of which waited for: 2 -> 1; matrix products, arithmetic and copies ran while one was open for 0% -> 0% of each run, Pallas kernels for 1% -> 0%
where the time goes in v4:
time: 125 us; the launch traced here: 124 us
  blocking collectives  93.3 us (75%)
  starting transfers between devices  22.1 us (18%)
  Pallas kernels  6.48 us (5%)
  waiting for transfers between devices  1.75 us (1%)
    all_to_all x4, blocking collectives, swap(): return lax.all_to_all(blocks, axis, split_axis=0, concat_axis=0, tiled=True)  73.8 us
    all_gather x1, blocking collectives, local(): low_parts = lax.all_gather(low_part, 'tp')  19.5 us
    all_to_all x1, starting transfers between devices, swap(): return lax.all_to_all(blocks, axis, split_axis=0, concat_axis=0, tiled=True)  14.9 us
    ppermute x2, starting transfers between devices, shifted(): lax.ppermute(shard, 'pair', [(i, (i + by) % devices) for i in range(devic...  7.14 us
    pallas_call x7, Pallas kernels, call(): pl.pallas_call(body, out_shape=out_shape, grid_spec=pltpu.PrefetchScalarG...  6.48 us
  transfers between devices with their start and end apart: 3, of which 1 were waited for; matrix products, arithmetic and copies ran while one was open for 0% of the time, Pallas kernels for 0%

profile of v4, /device:TPU:8, one launch (start us, length us, event | category | flops | bytes accessed | tf_op | source)
XLA Modules:
  0.0 124.3 jit_solution(2671556458092645030)
XLA Ops:
  0.6 2.9 %shard_map.112 = (bf16[128,128]{1,0:T(8,128)(2,1)}, bf16[32,2,2,2944]{3,2,1,0:T(2,128)(2,1)}, f32[64,128]{1,0:T(8,128)}) custom-call(s32[1]{0:T(128)} %bitcast.me, s32[64,1,128]{2,1,0:T(1,128)} %bitcast.13, s32[1,4]{1,0:T(1,128)} %window.1, bf16[128,640]{1,0:T(8,128)(2,1)} %key.1, bf16[128,640]{1,0:T(8,128)(2,1)} %value.1, bf16[128,640]{1,0:T(8,128)(2,1)} %refs_0_.3, ...), custom_call_target="tpu_custom_call" | custom-call | tf_op jit(solution)/shard_map/pallas_call | solution.py:44
  3.5 0.0 copy-start.3
  3.5 14.9 %all-to-all-start = ((bf16[64,2,2944]{2,1,0:T(2,128)(2,1)}), bf16[64,2,2944]{2,1,0:T(2,128)(2,1)S(1)}, u32[]{:S(2)}, u32[]{:S(2)}) async-start(bf16[64,2,2944]{2,1,0:T(2,128)(2,1)} %bitcast.11), calls=%async_computation | async-start | bytes 1507328 | tf_op jit(solution)/shard_map/all_to_all | solution.py:36
  18.5 0.0 copy-start
  18.5 0.0 copy-done.3
  18.5 0.0 copy-start.1
  18.5 19.5 %all-gather = f32[512,128]{1,0:T(8,128)S(1)} all-gather(f32[64,128]{1,0:T(8,128)S(1)} %copy-done.3), channel_id=2, replica_groups=mesh['pair'=32,'lane'=2,'tp'=8] {'tp'}, dimensions={0}, use_global_device_ids=true | all-gather | bytes 294912 | tf_op jit(solution)/shard_map/all_gather | solution.py:322
  38.0 0.0 copy-done
  38.0 0.0 copy-done.1
  38.0 0.3 shard_map.113.after
  38.3 1.7 %all-to-all-done.received.first = bf16[64,2,2944]{2,1,0:T(2,128)(2,1)S(1)} async-done(((bf16[64,2,2944]{2,1,0:T(2,128)(2,1)}), bf16[64,2,2944]{2,1,0:T(2,128)(2,1)S(1)}, u32[]{:S(2)}, u32[]{:S(2)}) %all-to-all-start) | async-done | bytes 753696 | tf_op jit(solution)/shard_map/all_to_all | solution.py:36
  40.1 0.1 shard_map.114.centre
  40.2 5.2 %collective-permute-start.1 = (bf16[256,768]{1,0:T(8,128)(2,1)S(1)}, bf16[256,768]{1,0:T(8,128)(2,1)S(1)}, u32[]{:S(2)}, u32[]{:S(2)}) collective-permute-start(bf16[256,768]{1,0:T(8,128)(2,1)S(1)} %shard_map.114.centre), channel_id=1, source_target_pairs={{0,496},{16,0},{32,16},{48,32},{64,48},{80,64},{96,80},{112,96},{1... | collective-permute-start | bytes 1179656 | tf_op jit(solution)/shard_map/ppermute | solution.py:32
  45.4 1.9 %collective-permute-start = (bf16[256,768]{1,0:T(8,128)(2,1)S(1)}, bf16[256,768]{1,0:T(8,128)(2,1)S(1)}, u32[]{:S(2)}, u32[]{:S(2)}) collective-permute-start(bf16[256,768]{1,0:T(8,128)(2,1)S(1)} %shard_map.114.centre), channel_id=1, source_target_pairs={{0,16},{16,32},{32,48},{48,64},{64,80},{80,96},{96,112},{112,128},... | collective-permute-start | bytes 1179656 | tf_op jit(solution)/shard_map/ppermute | solution.py:32
  47.3 0.0 copy-start.2
  47.4 21.5 %all_to_all.25.second = bf16[64,2,768]{2,1,0:T(2,128)(2,1)S(1)} all-to-all(bf16[64,2,768]{2,1,0:T(2,128)(2,1)S(1)} %bitcast.9), channel_id=1, replica_groups=mesh['pair'=32,'lane'=2,'tp'=8] {'pair','lane'}, dimensions={0} | all-to-all | bytes 393216 | tf_op jit(solution)/shard_map/all_to_all | solution.py:36
  68.9 0.0 collective-permute-done.1.right
  68.9 0.0 collective-permute-done.left
  68.9 0.0 copy-done.2
  68.9 1.8 %shard_map.115 = (bf16[128,640]{1,0:T(8,128)(2,1)S(1)}, bf16[16,64,128]{2,1,0:T(8,128)(2,1)S(1)}, f32[64,640]{1,0:T(8,128)S(1)}) custom-call(s32[1]{0:T(128)} %bitcast.me, bf16[256,768]{1,0:T(8,128)(2,1)S(1)} %collective-permute-done.left, bf16[256,768]{1,0:T(8,128)(2,1)S(1)} %collective-permute-done.1.right, bf16[256,768]{1,0:T(8,128)(2,1)S(1)} %shard_map.114.centre, ...), custom_call_target="tpu_custom_call" | custom-call | tf_op jit(solution)/shard_map/pallas_call | solution.py:44
  70.8 15.9 %all_to_all.26.parts = bf16[16,64,128]{2,1,0:T(8,128)(2,1)S(1)} all-to-all(bf16[16,64,128]{2,1,0:T(8,128)(2,1)S(1)} %get-tuple-element.15), channel_id=1, replica_groups=mesh['pair'=32,'lane'=2,'tp'=8] {'lane','tp'}, dimensions={0} | all-to-all | bytes 524288 | tf_op jit(solution)/shard_map/all_to_all | solution.py:36
  86.7 0.2 shard_map.116
  86.9 19.4 %all_to_all.27.received = bf16[64,2,1280]{2,1,0:T(2,128)(2,1)S(1)} all-to-all(bf16[64,2,1280]{2,1,0:T(2,128)(2,1)S(1)} %shard_map.116), channel_id=1, replica_groups=mesh['pair'=32,'lane'=2,'tp'=8] {'pair','lane'}, dimensions={0} | all-to-all | bytes 655360 | tf_op jit(solution)/shard_map/all_to_all | solution.py:36
  106.2 0.2 shard_map.117
  106.5 17.0 %all_to_all.28.totals = bf16[64,2,640]{2,1,0:T(2,128)(2,1)S(1)} all-to-all(bf16[64,2,640]{2,1,0:T(2,128)(2,1)S(1)} %shard_map.117), channel_id=1, replica_groups=mesh['pair'=32,'lane'=2,'tp'=8] {'pair','lane'}, dimensions={0} | all-to-all | bytes 327680 | tf_op jit(solution)/shard_map/all_to_all | solution.py:36
  123.4 0.9 shard_map.118
Async XLA Ops:
  3.5 15.0 %copy-start.3 = (f32[64,128]{1,0:T(8,128)S(1)}, f32[64,128]{1,0:T(8,128)}, u32[]{:S(2)}) copy-start(f32[64,128]{1,0:T(8,128)} %get-tuple-element.14) | copy-start | bytes 98308
  3.5 36.5 %all-to-all-start = ((bf16[64,2,2944]{2,1,0:T(2,128)(2,1)}), bf16[64,2,2944]{2,1,0:T(2,128)(2,1)S(1)}, u32[]{:S(2)}, u32[]{:S(2)}) async-start(bf16[64,2,2944]{2,1,0:T(2,128)(2,1)} %bitcast.11), calls=%async_computation | async-start | bytes 1507328 | tf_op jit(solution)/shard_map/all_to_all | solution.py:36
  18.5 19.6 %copy-start = (bf16[128,640]{1,0:T(8,128)(2,1)S(1)}, bf16[128,640]{1,0:T(8,128)(2,1)}, u32[]{:S(2)}) copy-start(bf16[128,640]{1,0:T(8,128)(2,1)} %refs_0_.3) | copy-start | bytes 491524
  18.5 19.5 %copy-start.1 = (bf16[128,128]{1,0:T(8,128)(2,1)S(1)}, bf16[128,128]{1,0:T(8,128)(2,1)}, u32[]{:S(2)}) copy-start(bf16[128,128]{1,0:T(8,128)(2,1)} %get-tuple-element.12.order) | copy-start | bytes 98308
  40.2 28.7 %collective-permute-start.1 = (bf16[256,768]{1,0:T(8,128)(2,1)S(1)}, bf16[256,768]{1,0:T(8,128)(2,1)S(1)}, u32[]{:S(2)}, u32[]{:S(2)}) collective-permute-start(bf16[256,768]{1,0:T(8,128)(2,1)S(1)} %shard_map.114.centre), channel_id=1, source_target_pairs={{0,496},{16,0},{32,16},{48,32},{64,48},{80,64},{96,80},{112,96},{1... | collective-permute-start | bytes 1179656 | tf_op jit(solution)/shard_map/ppermute | solution.py:32
  45.4 23.5 %collective-permute-start = (bf16[256,768]{1,0:T(8,128)(2,1)S(1)}, bf16[256,768]{1,0:T(8,128)(2,1)S(1)}, u32[]{:S(2)}, u32[]{:S(2)}) collective-permute-start(bf16[256,768]{1,0:T(8,128)(2,1)S(1)} %shard_map.114.centre), channel_id=1, source_target_pairs={{0,16},{16,32},{32,48},{48,64},{64,80},{80,96},{96,112},{112,128},... | collective-permute-start | bytes 1179656 | tf_op jit(solution)/shard_map/ppermute | solution.py:32
  47.3 21.6 %copy-start.2 = (bf16[64,640]{1,0:T(8,128)(2,1)S(1)}, bf16[64,640]{1,0:T(8,128)(2,1)}, u32[]{:S(2)}) copy-start(bf16[64,640]{1,0:T(8,128)(2,1)} %up.1) | copy-start | bytes 245764

commit v5 on v4

--- a/solution.py
+++ b/solution.py
@@ -16,6 +16,8 @@
 VMEM_BYTES = 48 * 1024 * 1024
 START_BYTES = 60 * 1024 * 1024
 SEQ = ("pair", "lane")
+TP = ("chip", "core")
+CORES = 2
 HEADS_OF = ((0, 1, 2), (3, 4, 2))
 UNITS = ((0, 0), (0, 1), (1, 0), (1, 1), (2, None))
 NT = (((1,), (1,)), ((), ()))
@@ -225,12 +227,20 @@
             ]
         else:
             low_of[tile] = low_of[tile] + low_grad
-    group = low_parts.shape[0] // 2
-    for k in range(low_parts.shape[0]):
-        low_parts[k] = low_of[k // group].astype(low_parts.dtype)
+    for tile in range(2):
+        low_parts[tile] = low_of[tile]
     for h in range(up_part.shape[1] // HEAD_DIM):
         halves = [up_of[heads.index(h)] if h in heads else jnp.zeros_like(up_of[0]) for heads in HEADS_OF]
         up_part[:, h * HEAD_DIM : (h + 1) * HEAD_DIM] = jnp.where(own, halves[0], halves[1])
+
+
+def chip_kernel(parts, send):
+    lanes = parts.shape[1]
+    chips = send.shape[0] // lanes
+    for tile in range(lanes):
+        total = (parts[0, tile] + parts[1, tile]).astype(send.dtype)
+        for k in range(chips):
+            send[tile * chips + k] = total
 
 
 def down_kernel(parts, second, out, up_part, send):
@@ -289,7 +299,7 @@
     tiles = lax.axis_size(SEQ)
     lanes = lax.axis_size("lane")
     pairs = tiles // lanes
-    group = lax.axis_size("tp")
+    group = lax.axis_size(TP)
     peer = tokens // tiles
     shared = len(HEADS_OF[0]) * HEAD_DIM
     bf16, f32 = jnp.bfloat16, jnp.float32
@@ -319,7 +329,7 @@
         START_BYTES,
     )
     first = swap(send.reshape(tiles, peer, columns), SEQ)
-    low_parts = lax.all_gather(low_part, "tp")
+    low_parts = lax.all_gather(jnp.sum(lax.all_gather(low_part, "core"), axis=0), "chip")
     second_width = len(SECOND) * width + 2 * rank
     second_send = call(
         second_kernel,
@@ -338,11 +348,17 @@
     second = swap(second_send.reshape(tiles, peer, second_width), SEQ)
     out_tile, low_grad_parts, up_part = call(
         attend_kernel,
-        [shape((tokens, width), bf16), shape((lanes * group, rank, tokens), bf16), shape((rank, width), f32)],
+        [shape((tokens, width), bf16), shape((lanes, rank, tokens), f32), shape((rank, width), f32)],
         (me,),
         (left, right, centre, first, second, adapter_up),
     )
-    low_grad_parts = swap(low_grad_parts, ("lane", "tp"))
+    low_grad_parts = call(
+        chip_kernel,
+        shape((lanes * group // CORES, rank, tokens), bf16),
+        (),
+        (lax.all_gather(low_grad_parts, "core"),),
+    )
+    low_grad_parts = swap(low_grad_parts, ("lane", "chip"))
     back_send = call(
         down_kernel,
         shape((tiles, peer, 2 * width), bf16),
@@ -365,18 +381,20 @@
     lanes = len(HEADS_OF)
     return jax.shard_map(
         local,
-        mesh=Mesh(mesh.devices.reshape(tiles // lanes, lanes, group), ("pair", "lane", "tp")),
+        mesh=Mesh(
+            mesh.devices.reshape(tiles // lanes, lanes, group // CORES, CORES), ("pair", "lane", "chip", "core")
+        ),
         in_specs=(
-            P(SEQ, "tp"),
-            P(SEQ, "tp"),
-            P(SEQ, "tp"),
-            P(SEQ, "tp"),
-            P(SEQ, "tp"),
-            P("tp", None),
-            P(None, "tp"),
+            P(SEQ, TP),
+            P(SEQ, TP),
+            P(SEQ, TP),
+            P(SEQ, TP),
+            P(SEQ, TP),
+            P(TP, None),
+            P(None, TP),
             P(),
             P(SEQ, None),
         ),
-        out_specs=(P(SEQ, "tp"), P("tp", None), P(None, "tp")),
+        out_specs=(P(SEQ, TP), P(TP, None), P(None, TP)),
         check_vma=False,
     )

time: 125 us -> 120 us (0.960)
  blocking collectives: 93.3 us -> 88.8 us
    all_to_all x4, blocking collectives: 73.8 us -> 68.2 us  [swap(): return lax.all_to_all(blocks, axis, split_axis=0, concat_axis=0, tiled=True)]
    all_gather x1 -> x3, blocking collectives: 19.5 us -> 20.6 us  [the longest x1 16.7 us: local(): lax.all_gather(jnp.sum(lax.all_gather(low_part, 'core'), axis=0), 'chip')]
    pallas_call x7 -> x8, Pallas kernels: 6.48 us -> 6.46 us  [call(): pl.pallas_call(body, out_shape=out_shape, grid_spec=pltpu.PrefetchScalarG...]
where the time goes in v5:
time: 120 us
  blocking collectives  88.8 us (74%)
  starting transfers between devices  21.2 us (18%)
  Pallas kernels  6.46 us (5%)
  waiting for transfers between devices  2.59 us (2%)
    all_to_all x4, blocking collectives, swap(): return lax.all_to_all(blocks, axis, split_axis=0, concat_axis=0, tiled=True)  68.2 us
    all_gather x1, blocking collectives, local(): lax.all_gather(jnp.sum(lax.all_gather(low_part, 'core'), axis=0), 'chip')  16.7 us
    all_to_all x1, starting transfers between devices, swap(): return lax.all_to_all(blocks, axis, split_axis=0, concat_axis=0, tiled=True)  14.9 us
    pallas_call x8, Pallas kernels, call(): pl.pallas_call(body, out_shape=out_shape, grid_spec=pltpu.PrefetchScalarG...  6.46 us
    ppermute x2, starting transfers between devices, shifted(): lax.ppermute(shard, 'pair', [(i, (i + by) % devices) for i in range(devic...  6.28 us
    all_to_all x1, waiting for transfers between devices, swap(): return lax.all_to_all(blocks, axis, split_axis=0, concat_axis=0, tiled=True)  2.59 us
  transfers between devices with their start and end apart: 3, of which 1 were waited for; matrix products, arithmetic and copies ran while one was open for 0% of the time, Pallas kernels for 0%

profile of v5, /device:TPU:8, one launch (start us, length us, event | category | flops | bytes accessed | tf_op | source)
XLA Modules:
  0.0 119.8 jit_solution(18109420043056667779)
XLA Ops:
  0.6 2.9 %shard_map.112 = (bf16[128,128]{1,0:T(8,128)(2,1)}, bf16[32,2,2,2944]{3,2,1,0:T(2,128)(2,1)}, f32[64,128]{1,0:T(8,128)}) custom-call(s32[1]{0:T(128)} %bitcast.me, s32[64,1,128]{2,1,0:T(1,128)} %bitcast.17, s32[1,4]{1,0:T(1,128)} %window.1, bf16[128,640]{1,0:T(8,128)(2,1)} %key.1, bf16[128,640]{1,0:T(8,128)(2,1)} %value.1, bf16[128,640]{1,0:T(8,128)(2,1)} %refs_0_.3, ...), custom_call_target="tpu_custom_call" | custom-call | tf_op jit(solution)/shard_map/pallas_call | solution.py:46
  3.5 0.0 copy-start.3
  3.5 14.9 %all-to-all-start = ((bf16[64,2,2944]{2,1,0:T(2,128)(2,1)}), bf16[64,2,2944]{2,1,0:T(2,128)(2,1)S(1)}, u32[]{:S(2)}, u32[]{:S(2)}) async-start(bf16[64,2,2944]{2,1,0:T(2,128)(2,1)} %bitcast.14), calls=%async_computation | async-start | bytes 1507328 | tf_op jit(solution)/shard_map/all_to_all | solution.py:38
  18.5 0.0 copy-done.3
  18.5 0.0 copy-start
  18.5 2.0 %all-gather = f32[128,128]{1,0:T(8,128)S(1)} all-gather(f32[64,128]{1,0:T(8,128)S(1)} %copy-done.3), channel_id=2, replica_groups=mesh['pair'=32,'lane'=2,'chip'=4,'core'=2] {'core'}, dimensions={0}, use_global_device_ids=true | all-gather | bytes 98304 | tf_op jit(solution)/shard_map/all_gather | solution.py:332
  20.5 0.0 copy-start.1
  20.5 16.7 %all-gather.1 = f32[256,128]{1,0:T(8,128)S(1)} all-gather(f32[64,128]{1,0:T(8,128)S(1)} %reduce_sum.9), channel_id=3, replica_groups=mesh['pair'=32,'lane'=2,'chip'=4,'core'=2] {'chip'}, dimensions={0}, use_global_device_ids=true | all-gather | bytes 163840 | tf_op jit(solution)/shard_map/all_gather | solution.py:332
  37.2 0.0 copy-done
  37.2 0.0 copy-done.1
  37.2 0.3 shard_map.113.after
  37.5 2.6 %all-to-all-done.received.first = bf16[64,2,2944]{2,1,0:T(2,128)(2,1)S(1)} async-done(((bf16[64,2,2944]{2,1,0:T(2,128)(2,1)}), bf16[64,2,2944]{2,1,0:T(2,128)(2,1)S(1)}, u32[]{:S(2)}, u32[]{:S(2)}) %all-to-all-start) | async-done | bytes 753696 | tf_op jit(solution)/shard_map/all_to_all | solution.py:38
  40.1 0.1 shard_map.114.centre
  40.2 4.4 %collective-permute-start.1 = (bf16[256,768]{1,0:T(8,128)(2,1)S(1)}, bf16[256,768]{1,0:T(8,128)(2,1)S(1)}, u32[]{:S(2)}, u32[]{:S(2)}) collective-permute-start(bf16[256,768]{1,0:T(8,128)(2,1)S(1)} %shard_map.114.centre), channel_id=1, source_target_pairs={{0,496},{16,0},{32,16},{48,32},{64,48},{80,64},{96,80},{112,96},{1... | collective-permute-start | bytes 1179656 | tf_op jit(solution)/shard_map/ppermute | solution.py:34
  44.6 1.9 %collective-permute-start = (bf16[256,768]{1,0:T(8,128)(2,1)S(1)}, bf16[256,768]{1,0:T(8,128)(2,1)S(1)}, u32[]{:S(2)}, u32[]{:S(2)}) collective-permute-start(bf16[256,768]{1,0:T(8,128)(2,1)S(1)} %shard_map.114.centre), channel_id=1, source_target_pairs={{0,16},{16,32},{32,48},{48,64},{64,80},{80,96},{96,112},{112,128},... | collective-permute-start | bytes 1179656 | tf_op jit(solution)/shard_map/ppermute | solution.py:34
  46.5 0.0 copy-start.2
  46.5 20.9 %all_to_all.25.second = bf16[64,2,768]{2,1,0:T(2,128)(2,1)S(1)} all-to-all(bf16[64,2,768]{2,1,0:T(2,128)(2,1)S(1)} %bitcast.11), channel_id=1, replica_groups=mesh['pair'=32,'lane'=2,'chip'=4,'core'=2] {'pair','lane'}, dimensions={0} | all-to-all | bytes 393216 | tf_op jit(solution)/shard_map/all_to_all | solution.py:38
  67.4 0.0 collective-permute-done.1.right
  67.4 0.0 collective-permute-done.left
  67.4 0.0 copy-done.2
  67.4 1.8 %shard_map.115 = (bf16[128,640]{1,0:T(8,128)(2,1)S(1)}, f32[2,64,128]{2,1,0:T(8,128)S(1)}, f32[64,640]{1,0:T(8,128)S(1)}) custom-call(s32[1]{0:T(128)} %bitcast.me, bf16[256,768]{1,0:T(8,128)(2,1)S(1)} %collective-permute-done.left, bf16[256,768]{1,0:T(8,128)(2,1)S(1)} %collective-permute-done.1.right, bf16[256,768]{1,0:T(8,128)(2,1)S(1)} %shard_map.114.centre, ...), custom_call_target="tpu_custom_call" | custom-call | tf_op jit(solution)/shard_map/pallas_call | solution.py:46
  69.3 1.9 %all-gather.2 = f32[4,64,128]{2,1,0:T(8,128)S(1)} all-gather(f32[2,64,128]{2,1,0:T(8,128)S(1)} %get-tuple-element.15), channel_id=4, replica_groups=mesh['pair'=32,'lane'=2,'chip'=4,'core'=2] {'core'}, dimensions={0}, use_global_device_ids=true | all-gather | bytes 196608 | tf_op jit(solution)/shard_map/all_gather | solution.py:359
  71.2 14.0 %all_to_all.26.parts = bf16[8,64,128]{2,1,0:T(8,128)(2,1)S(1)} all-to-all(bf16[8,64,128]{2,1,0:T(8,128)(2,1)S(1)} %shard_map.116), channel_id=1, replica_groups=mesh['pair'=32,'lane'=2,'chip'=4,'core'=2] {'lane','chip'}, dimensions={0} | all-to-all | bytes 262144 | tf_op jit(solution)/shard_map/all_to_all | solution.py:38
  85.2 0.2 shard_map.117
  85.4 17.8 %all_to_all.27.received = bf16[64,2,1280]{2,1,0:T(2,128)(2,1)S(1)} all-to-all(bf16[64,2,1280]{2,1,0:T(2,128)(2,1)S(1)} %shard_map.117), channel_id=1, replica_groups=mesh['pair'=32,'lane'=2,'chip'=4,'core'=2] {'pair','lane'}, dimensions={0} | all-to-all | bytes 655360 | tf_op jit(solution)/shard_map/all_to_all | solution.py:38
  103.1 0.2 shard_map.118
  103.3 15.5 %all_to_all.28.totals = bf16[64,2,640]{2,1,0:T(2,128)(2,1)S(1)} all-to-all(bf16[64,2,640]{2,1,0:T(2,128)(2,1)S(1)} %shard_map.118), channel_id=1, replica_groups=mesh['pair'=32,'lane'=2,'chip'=4,'core'=2] {'pair','lane'}, dimensions={0} | all-to-all | bytes 327680 | tf_op jit(solution)/shard_map/all_to_all | solution.py:38
  118.8 0.9 shard_map.119
  (2 shorter events, 0.0 us)
Async XLA Ops:
  3.5 14.9 %copy-start.3 = (f32[64,128]{1,0:T(8,128)S(1)}, f32[64,128]{1,0:T(8,128)}, u32[]{:S(2)}) copy-start(f32[64,128]{1,0:T(8,128)} %get-tuple-element.14) | copy-start | bytes 98308
  3.5 36.5 %all-to-all-start = ((bf16[64,2,2944]{2,1,0:T(2,128)(2,1)}), bf16[64,2,2944]{2,1,0:T(2,128)(2,1)S(1)}, u32[]{:S(2)}, u32[]{:S(2)}) async-start(bf16[64,2,2944]{2,1,0:T(2,128)(2,1)} %bitcast.14), calls=%async_computation | async-start | bytes 1507328 | tf_op jit(solution)/shard_map/all_to_all | solution.py:38
  18.5 18.7 %copy-start = (bf16[128,640]{1,0:T(8,128)(2,1)S(1)}, bf16[128,640]{1,0:T(8,128)(2,1)}, u32[]{:S(2)}) copy-start(bf16[128,640]{1,0:T(8,128)(2,1)} %refs_0_.3) | copy-start | bytes 491524
  20.5 16.7 %copy-start.1 = (bf16[128,128]{1,0:T(8,128)(2,1)S(1)}, bf16[128,128]{1,0:T(8,128)(2,1)}, u32[]{:S(2)}) copy-start(bf16[128,128]{1,0:T(8,128)(2,1)} %get-tuple-element.12.order) | copy-start | bytes 98308
  40.2 27.2 %collective-permute-start.1 = (bf16[256,768]{1,0:T(8,128)(2,1)S(1)}, bf16[256,768]{1,0:T(8,128)(2,1)S(1)}, u32[]{:S(2)}, u32[]{:S(2)}) collective-permute-start(bf16[256,768]{1,0:T(8,128)(2,1)S(1)} %shard_map.114.centre), channel_id=1, source_target_pairs={{0,496},{16,0},{32,16},{48,32},{64,48},{80,64},{96,80},{112,96},{1... | collective-permute-start | bytes 1179656 | tf_op jit(solution)/shard_map/ppermute | solution.py:34
  44.6 22.9 %collective-permute-start = (bf16[256,768]{1,0:T(8,128)(2,1)S(1)}, bf16[256,768]{1,0:T(8,128)(2,1)S(1)}, u32[]{:S(2)}, u32[]{:S(2)}) collective-permute-start(bf16[256,768]{1,0:T(8,128)(2,1)S(1)} %shard_map.114.centre), channel_id=1, source_target_pairs={{0,16},{16,32},{32,48},{48,64},{64,80},{80,96},{96,112},{112,128},... | collective-permute-start | bytes 1179656 | tf_op jit(solution)/shard_map/ppermute | solution.py:34
  46.5 21.0 %copy-start.2 = (bf16[64,640]{1,0:T(8,128)(2,1)S(1)}, bf16[64,640]{1,0:T(8,128)(2,1)}, u32[]{:S(2)}) copy-start(bf16[64,640]{1,0:T(8,128)(2,1)} %up.1) | copy-start | bytes 245764

commit v6 on v5

--- a/solution.py
+++ b/solution.py
@@ -234,13 +234,13 @@
         up_part[:, h * HEAD_DIM : (h + 1) * HEAD_DIM] = jnp.where(own, halves[0], halves[1])
 
 
-def chip_kernel(parts, send):
-    lanes = parts.shape[1]
-    chips = send.shape[0] // lanes
-    for tile in range(lanes):
-        total = (parts[0, tile] + parts[1, tile]).astype(send.dtype)
-        for k in range(chips):
-            send[tile * chips + k] = total
+def chip_kernel(me, parts, send):
+    lane = lax.rem(me[0], 2)
+    total = parts[0, lane]
+    for k in range(1, parts.shape[0]):
+        total = total + parts[k, lane]
+    for k in range(send.shape[0]):
+        send[k] = total.astype(send.dtype)
 
 
 def down_kernel(parts, second, out, up_part, send):
@@ -354,11 +354,11 @@
     )
     low_grad_parts = call(
         chip_kernel,
-        shape((lanes * group // CORES, rank, tokens), bf16),
-        (),
-        (lax.all_gather(low_grad_parts, "core"),),
-    )
-    low_grad_parts = swap(low_grad_parts, ("lane", "chip"))
+        shape((group // CORES, rank, tokens), bf16),
+        (me,),
+        (lax.all_gather(low_grad_parts, ("lane", "core")),),
+    )
+    low_grad_parts = swap(low_grad_parts, "chip")
     back_send = call(
         down_kernel,
         shape((tiles, peer, 2 * width), bf16),

time: 120 us -> 124 us (1.033)
  blocking collectives: 88.8 us -> 92.9 us
    all_gather x1, blocking collectives: 1.9 us -> 5.79 us  [local(): lax.all_gather(low_grad_parts, ('lane', 'core'))]
where the time goes in v6:
time: 124 us
  blocking collectives  92.9 us (75%)
  starting transfers between devices  21.2 us (17%)
  Pallas kernels  6.46 us (5%)
  waiting for transfers between devices  2.59 us (2%)
    all_to_all x4, blocking collectives, swap(): return lax.all_to_all(blocks, axis, split_axis=0, concat_axis=0, tiled=True)  68.4 us
    all_gather x1, blocking collectives, local(): lax.all_gather(jnp.sum(lax.all_gather(low_part, 'core'), axis=0), 'chip')  16.7 us
    all_to_all x1, starting transfers between devices, swap(): return lax.all_to_all(blocks, axis, split_axis=0, concat_axis=0, tiled=True)  14.9 us
    pallas_call x8, Pallas kernels, call(): pl.pallas_call(body, out_shape=out_shape, grid_spec=pltpu.PrefetchScalarG...  6.46 us
    ppermute x2, starting transfers between devices, shifted(): lax.ppermute(shard, 'pair', [(i, (i + by) % devices) for i in range(devic...  6.28 us
    all_gather x1, blocking collectives, local(): lax.all_gather(low_grad_parts, ('lane', 'core'))  5.79 us
    all_to_all x1, waiting for transfers between devices, swap(): return lax.all_to_all(blocks, axis, split_axis=0, concat_axis=0, tiled=True)  2.59 us
  transfers between devices with their start and end apart: 3, of which 1 were waited for; matrix products, arithmetic and copies ran while one was open for 0% of the time, Pallas kernels for 0%

profile of v6, /device:TPU:8, one launch (start us, length us, event | category | flops | bytes accessed | tf_op | source)
XLA Modules:
  0.0 123.9 jit_solution(2064899652040759978)
XLA Ops:
  0.6 2.9 %shard_map.112 = (bf16[128,128]{1,0:T(8,128)(2,1)}, bf16[32,2,2,2944]{3,2,1,0:T(2,128)(2,1)}, f32[64,128]{1,0:T(8,128)}) custom-call(s32[1]{0:T(128)} %bitcast.me, s32[64,1,128]{2,1,0:T(1,128)} %bitcast.17, s32[1,4]{1,0:T(1,128)} %window.1, bf16[128,640]{1,0:T(8,128)(2,1)} %key.1, bf16[128,640]{1,0:T(8,128)(2,1)} %value.1, bf16[128,640]{1,0:T(8,128)(2,1)} %refs_0_.3, ...), custom_call_target="tpu_custom_call" | custom-call | tf_op jit(solution)/shard_map/pallas_call | solution.py:46
  3.5 0.0 copy-start.3
  3.5 14.9 %all-to-all-start = ((bf16[64,2,2944]{2,1,0:T(2,128)(2,1)}), bf16[64,2,2944]{2,1,0:T(2,128)(2,1)S(1)}, u32[]{:S(2)}, u32[]{:S(2)}) async-start(bf16[64,2,2944]{2,1,0:T(2,128)(2,1)} %bitcast.14), calls=%async_computation | async-start | bytes 1507328 | tf_op jit(solution)/shard_map/all_to_all | solution.py:38
  18.5 0.0 copy-done.3
  18.5 0.0 copy-start
  18.5 2.0 %all-gather = f32[128,128]{1,0:T(8,128)S(1)} all-gather(f32[64,128]{1,0:T(8,128)S(1)} %copy-done.3), channel_id=2, replica_groups=mesh['pair'=32,'lane'=2,'chip'=4,'core'=2] {'core'}, dimensions={0}, use_global_device_ids=true | all-gather | bytes 98304 | tf_op jit(solution)/shard_map/all_gather | solution.py:332
  20.5 0.0 copy-start.1
  20.5 16.7 %all-gather.1 = f32[256,128]{1,0:T(8,128)S(1)} all-gather(f32[64,128]{1,0:T(8,128)S(1)} %reduce_sum.9), channel_id=3, replica_groups=mesh['pair'=32,'lane'=2,'chip'=4,'core'=2] {'chip'}, dimensions={0}, use_global_device_ids=true | all-gather | bytes 163840 | tf_op jit(solution)/shard_map/all_gather | solution.py:332
  37.2 0.0 copy-done
  37.2 0.0 copy-done.1
  37.2 0.3 shard_map.113.after
  37.5 2.6 %all-to-all-done.received.first = bf16[64,2,2944]{2,1,0:T(2,128)(2,1)S(1)} async-done(((bf16[64,2,2944]{2,1,0:T(2,128)(2,1)}), bf16[64,2,2944]{2,1,0:T(2,128)(2,1)S(1)}, u32[]{:S(2)}, u32[]{:S(2)}) %all-to-all-start) | async-done | bytes 753696 | tf_op jit(solution)/shard_map/all_to_all | solution.py:38
  40.1 0.1 shard_map.114.centre
  40.2 4.4 %collective-permute-start.1 = (bf16[256,768]{1,0:T(8,128)(2,1)S(1)}, bf16[256,768]{1,0:T(8,128)(2,1)S(1)}, u32[]{:S(2)}, u32[]{:S(2)}) collective-permute-start(bf16[256,768]{1,0:T(8,128)(2,1)S(1)} %shard_map.114.centre), channel_id=1, source_target_pairs={{0,496},{16,0},{32,16},{48,32},{64,48},{80,64},{96,80},{112,96},{1... | collective-permute-start | bytes 1179656 | tf_op jit(solution)/shard_map/ppermute | solution.py:34
  44.6 1.9 %collective-permute-start = (bf16[256,768]{1,0:T(8,128)(2,1)S(1)}, bf16[256,768]{1,0:T(8,128)(2,1)S(1)}, u32[]{:S(2)}, u32[]{:S(2)}) collective-permute-start(bf16[256,768]{1,0:T(8,128)(2,1)S(1)} %shard_map.114.centre), channel_id=1, source_target_pairs={{0,16},{16,32},{32,48},{48,64},{64,80},{80,96},{96,112},{112,128},... | collective-permute-start | bytes 1179656 | tf_op jit(solution)/shard_map/ppermute | solution.py:34
  46.5 0.0 copy-start.2
  46.5 20.9 %all_to_all.25.second = bf16[64,2,768]{2,1,0:T(2,128)(2,1)S(1)} all-to-all(bf16[64,2,768]{2,1,0:T(2,128)(2,1)S(1)} %bitcast.11), channel_id=1, replica_groups=mesh['pair'=32,'lane'=2,'chip'=4,'core'=2] {'pair','lane'}, dimensions={0} | all-to-all | bytes 393216 | tf_op jit(solution)/shard_map/all_to_all | solution.py:38
  67.4 0.0 collective-permute-done.1.right
  67.4 0.0 collective-permute-done.left
  67.4 0.0 copy-done.2
  67.4 1.8 %shard_map.115 = (bf16[128,640]{1,0:T(8,128)(2,1)S(1)}, f32[2,64,128]{2,1,0:T(8,128)S(1)}, f32[64,640]{1,0:T(8,128)S(1)}) custom-call(s32[1]{0:T(128)} %bitcast.me, bf16[256,768]{1,0:T(8,128)(2,1)S(1)} %collective-permute-done.left, bf16[256,768]{1,0:T(8,128)(2,1)S(1)} %collective-permute-done.1.right, bf16[256,768]{1,0:T(8,128)(2,1)S(1)} %shard_map.114.centre, ...), custom_call_target="tpu_custom_call" | custom-call | tf_op jit(solution)/shard_map/pallas_call | solution.py:46
  69.3 5.8 %all-gather.2 = f32[8,64,128]{2,1,0:T(8,128)S(1)} all-gather(f32[2,64,128]{2,1,0:T(8,128)S(1)} %get-tuple-element.15), channel_id=4, replica_groups=mesh['pair'=32,'lane'=2,'chip'=4,'core'=2] {'lane','core'}, dimensions={0}, use_global_device_ids=true | all-gather | bytes 327680 | tf_op jit(solution)/shard_map/all_gather | solution.py:359
  75.1 13.8 %all_to_all.26.parts = bf16[4,64,128]{2,1,0:T(8,128)(2,1)S(1)} all-to-all(bf16[4,64,128]{2,1,0:T(8,128)(2,1)S(1)} %shard_map.116), channel_id=1, replica_groups=mesh['pair'=32,'lane'=2,'chip'=4,'core'=2] {'chip'}, dimensions={0} | all-to-all | bytes 131072 | tf_op jit(solution)/shard_map/all_to_all | solution.py:38
  88.9 0.2 shard_map.117
  89.0 18.1 %all_to_all.27.received = bf16[64,2,1280]{2,1,0:T(2,128)(2,1)S(1)} all-to-all(bf16[64,2,1280]{2,1,0:T(2,128)(2,1)S(1)} %shard_map.117), channel_id=1, replica_groups=mesh['pair'=32,'lane'=2,'chip'=4,'core'=2] {'pair','lane'}, dimensions={0} | all-to-all | bytes 655360 | tf_op jit(solution)/shard_map/all_to_all | solution.py:38
  107.2 0.2 shard_map.118
  107.4 15.6 %all_to_all.28.totals = bf16[64,2,640]{2,1,0:T(2,128)(2,1)S(1)} all-to-all(bf16[64,2,640]{2,1,0:T(2,128)(2,1)S(1)} %shard_map.118), channel_id=1, replica_groups=mesh['pair'=32,'lane'=2,'chip'=4,'core'=2] {'pair','lane'}, dimensions={0} | all-to-all | bytes 327680 | tf_op jit(solution)/shard_map/all_to_all | solution.py:38
  123.0 0.9 shard_map.119
  (2 shorter events, 0.0 us)
Async XLA Ops:
  3.5 14.9 %copy-start.3 = (f32[64,128]{1,0:T(8,128)S(1)}, f32[64,128]{1,0:T(8,128)}, u32[]{:S(2)}) copy-start(f32[64,128]{1,0:T(8,128)} %get-tuple-element.14) | copy-start | bytes 98308
  3.5 36.5 %all-to-all-start = ((bf16[64,2,2944]{2,1,0:T(2,128)(2,1)}), bf16[64,2,2944]{2,1,0:T(2,128)(2,1)S(1)}, u32[]{:S(2)}, u32[]{:S(2)}) async-start(bf16[64,2,2944]{2,1,0:T(2,128)(2,1)} %bitcast.14), calls=%async_computation | async-start | bytes 1507328 | tf_op jit(solution)/shard_map/all_to_all | solution.py:38
  18.5 18.7 %copy-start = (bf16[128,640]{1,0:T(8,128)(2,1)S(1)}, bf16[128,640]{1,0:T(8,128)(2,1)}, u32[]{:S(2)}) copy-start(bf16[128,640]{1,0:T(8,128)(2,1)} %refs_0_.3) | copy-start | bytes 491524
  20.5 16.7 %copy-start.1 = (bf16[128,128]{1,0:T(8,128)(2,1)S(1)}, bf16[128,128]{1,0:T(8,128)(2,1)}, u32[]{:S(2)}) copy-start(bf16[128,128]{1,0:T(8,128)(2,1)} %get-tuple-element.12.order) | copy-start | bytes 98308
  40.2 27.2 %collective-permute-start.1 = (bf16[256,768]{1,0:T(8,128)(2,1)S(1)}, bf16[256,768]{1,0:T(8,128)(2,1)S(1)}, u32[]{:S(2)}, u32[]{:S(2)}) collective-permute-start(bf16[256,768]{1,0:T(8,128)(2,1)S(1)} %shard_map.114.centre), channel_id=1, source_target_pairs={{0,496},{16,0},{32,16},{48,32},{64,48},{80,64},{96,80},{112,96},{1... | collective-permute-start | bytes 1179656 | tf_op jit(solution)/shard_map/ppermute | solution.py:34
  44.6 22.9 %collective-permute-start = (bf16[256,768]{1,0:T(8,128)(2,1)S(1)}, bf16[256,768]{1,0:T(8,128)(2,1)S(1)}, u32[]{:S(2)}, u32[]{:S(2)}) collective-permute-start(bf16[256,768]{1,0:T(8,128)(2,1)S(1)} %shard_map.114.centre), channel_id=1, source_target_pairs={{0,16},{16,32},{32,48},{48,64},{64,80},{80,96},{96,112},{112,128},... | collective-permute-start | bytes 1179656 | tf_op jit(solution)/shard_map/ppermute | solution.py:34
  46.5 21.0 %copy-start.2 = (bf16[64,640]{1,0:T(8,128)(2,1)S(1)}, bf16[64,640]{1,0:T(8,128)(2,1)}, u32[]{:S(2)}) copy-start(bf16[64,640]{1,0:T(8,128)(2,1)} %up.1) | copy-start | bytes 245764
